TPU v7x, 512 devices: a whole 4x8x8 slice. The times are simulated.
512 devices in a mesh: ctx: 64 (over z, x, y_hi), head: 8 (over y_lo, core).
Axes of the slice: x: 4, y: 8 (y_hi: 2, y_lo: 4; y = y_hi * 4 + y_lo), z: 8, core: 2. Of those that a mesh axis runs over, the one named last changes fastest.
Arguments:
- fresh_query: bfloat16 [1024, 3072], P('ctx', 'head'), may hold values from -64 to 64
- fresh_key: bfloat16 [1024, 3072], P('ctx', 'head'), may hold values from -2.5 to 2.5
- fresh_value: bfloat16 [1024, 3072], P('ctx', 'head'), may hold values from -6 to 6
- cache_key: bfloat16 [65536, 3072], P('ctx', 'head'), may hold values from -6 to 6
- cache_value: bfloat16 [65536, 3072], P('ctx', 'head'), may hold values from -6 to 6
- slot_owner: int32 [64], replicated, may hold values from 0 to 63, each once
- evictor: int32 [1], replicated, may hold values from 0 to 63
- timestep: int32 [1], replicated, may hold values from 0 to 49
- age_slope: float32 [24], P('head'), may hold values from 0.5 to 4
- time_gate: float32 [50, 3072], P(None, 'head'), may hold values from 0.5 to 2
Outputs:
- attn_output: bfloat16 [1024, 3072], P('ctx', 'head')
- next_key: bfloat16 [65536, 3072], P('ctx', 'head')
- next_value: bfloat16 [65536, 3072], P('ctx', 'head')
Inputs may be any that keep to these rules, and one draw needn't show every extreme that they name: `slot_owner`: a permutation of the 64 owners.
All inputs are finite; a program needn't handle non-finite values.
Results may differ from a plain program's by a relative error of at most 0.003.
Values may be sent and summed in bfloat16 or wider, within the bound.
No kernel may reach another device: no remote copies, remote signals or barrier semaphores. Data moves between devices by JAX's collectives and lax.ppermute only.
A program may use at most 64 MiB of HBM per device.

v0:
```python
import math

import jax
import jax.numpy as jnp
from jax import lax
from jax.sharding import PartitionSpec as P


def body(
    fresh_query,
    fresh_key,
    fresh_value,
    cache_key,
    cache_value,
    slot_owner,
    evictor,
    timestep,
    age_slope,
    time_gate,
):
    feature_width = fresh_query.shape[1]
    heads_here = age_slope.shape[0]
    head_dim = feature_width // heads_here
    owners = lax.axis_size("ctx")
    owner_index = lax.axis_index("ctx")
    queries = lax.all_gather(fresh_query, "ctx", axis=0, tiled=True)
    total_rows = queries.shape[0]
    block_rows = min(512, total_rows)
    blocks = total_rows // block_rows
    slot_ids = jnp.arange(owners, dtype=jnp.int32)
    slot_rank = jnp.sum(jnp.where(slot_owner == owner_index, slot_ids, 0))
    cache_age = (slot_rank + 1).astype(jnp.float32) / owners
    local_keys = jnp.concatenate([fresh_key, cache_key], 0)
    local_values = jnp.concatenate([fresh_value, cache_value], 0)
    key_count = local_keys.shape[0]
    key_age = jnp.where(jnp.arange(key_count) >= fresh_key.shape[0], cache_age, 0.0)
    penalty = (age_slope[:, None] * key_age[None, :])[:, None, :]
    head_keys = local_keys.reshape(key_count, heads_here, head_dim)
    head_values = local_values.reshape(key_count, heads_here, head_dim)
    query_blocks = queries.reshape(blocks, block_rows, heads_here, head_dim)
    score_scale = 1.0 / math.sqrt(head_dim)

    def weigh_block(query_block):
        scores = (
            jnp.einsum("qhd,khd->hqk", query_block, head_keys, preferred_element_type=jnp.float32)
            * score_scale
            - penalty
        )
        largest = jnp.max(scores, axis=2)
        weights = jnp.exp(scores - largest[:, :, None]).astype(jnp.bfloat16)
        denominator = jnp.sum(weights.astype(jnp.float32), axis=2)
        numerator = jnp.einsum(
            "hqk,khd->qhd", weights, head_values, preferred_element_type=jnp.float32
        )
        return (numerator.reshape(block_rows, feature_width), denominator.T, largest.T)

    numerators, denominators, maxima = lax.map(weigh_block, query_blocks)
    numerators = numerators.reshape(total_rows, feature_width)
    denominators = denominators.reshape(total_rows, heads_here)
    maxima = maxima.reshape(total_rows, heads_here)
    row_max = lax.pmax(maxima, "ctx")
    factor = jnp.exp(maxima - row_max)
    scaled_numer = (
        numerators.reshape(total_rows, heads_here, head_dim) * factor[:, :, None]
    ).reshape(total_rows, feature_width)
    scaled_denom = denominators * factor
    own_numer, own_denom = (
        lax.psum_scatter(scaled_numer, "ctx", scatter_dimension=0, tiled=True),
        lax.psum_scatter(scaled_denom, "ctx", scatter_dimension=0, tiled=True),
    )
    rows_here = own_numer.shape[0]
    own_numer = own_numer.reshape(rows_here, heads_here, head_dim)
    attended = (own_numer / own_denom[:, :, None]).reshape(rows_here, feature_width)
    squares = lax.psum(jnp.sum(attended * attended, axis=1), "head")
    inverse = lax.rsqrt(squares / (feature_width * lax.axis_size("head")) + 1e-06)
    picked = jnp.arange(time_gate.shape[0]) == timestep[0]
    gate_row = jnp.sum(jnp.where(picked[:, None], time_gate, 0.0), axis=0)
    attn_output = (attended * inverse[:, None] * gate_row[None, :]).astype(jnp.bfloat16)
    fresh_keys, fresh_values = (
        lax.all_gather(fresh_key, "ctx", axis=0, tiled=True),
        lax.all_gather(fresh_value, "ctx", axis=0, tiled=True),
    )
    evicted = owner_index == evictor[0]
    next_key = jnp.where(evicted, fresh_keys, cache_key)
    next_value = jnp.where(evicted, fresh_values, cache_value)
    return (attn_output, next_key, next_value)


def solution(mesh):
    return jax.shard_map(
        body,
        mesh=mesh,
        in_specs=(
            P("ctx", "head"),
            P("ctx", "head"),
            P("ctx", "head"),
            P("ctx", "head"),
            P("ctx", "head"),
            P(),
            P(),
            P(),
            P("head"),
            P(None, "head"),
        ),
        out_specs=(P("ctx", "head"), P("ctx", "head"), P("ctx", "head")),
        check_vma=False,
    )
```

profile of v0, /device:TPU:1, one launch (start us, length us, event | category | flops | bytes accessed | tf_op | source)
XLA Modules:
  0.0 2006.9 jit_solution(5464234785471531787)
XLA Ops:
  7.2 0.0 reduce-scatter.9.cloned.1.call-start
  7.3 1.3 fusion.7
  9.2 209.3 %all_gather.9 = bf16[1024,384]{1,0:T(8,128)(2,1)S(1)} all-gather(bf16[16,384]{1,0:T(8,128)(2,1)} %param.12), channel_id=1, replica_groups=mesh['ctx'=64,'head'=8] {'ctx'}, dimensions={0}, use_global_device_ids=true | all-gather | bytes 798720 | tf_op jit(solution)/shard_map/all_gather | solution.py:26
  218.5 0.2 reshape.87
  218.7 0.0 copy-start
  218.8 0.0 copy-start.4
  218.8 0.1 copy.30
  218.9 1.3 pad_maximum_fusion
  220.2 1.4 copy.28
  221.6 0.0 copy-start.6
  221.6 0.9 copy.31
  222.5 0.1 pad_maximum_fusion.1
  222.5 1.4 copy.29
  223.9 0.9 copy.32
  224.8 38.4 %while.15 = (s32[]{:T(128)}, f32[2,512,384]{1,0,2:T(2,128)}, f32[2,512,3]{1,2,0:T(4,128)S(1)}, f32[2,512,3]{1,2,0:T(4,128)S(1)}, bf16[2,512,3,128]{3,1,2,0:T(8,1...) while((s32[]{:T(128)}, f32[2,512,384]{1,0,2:T(2,128)}, ...), condition=%wide.region_4.5_spmd.clone, body=%wide.region_1.4_spmd.clone.sunk | while | flops 832266304 | bytes 25184644 | solution.py:57
  224.8 0.1 multiply_bitcast_fusion.2
  224.9 1.4 fusion.18
  226.3 0.9 convert_reduce_fusion.2
  227.2 1.2 fusion.19
  228.3 0.8 copy.54
  229.2 14.8 dynamic_update_slice.19
  244.0 0.1 multiply_bitcast_fusion.2
  244.1 1.4 fusion.18
  245.5 0.9 convert_reduce_fusion.2
  246.4 1.2 fusion.19
  247.5 0.8 copy.54
  248.3 14.8 dynamic_update_slice.19
  263.2 374.3 %pmax.7 = f32[1024,3]{0,1:T(4,128)S(1)} all-reduce(f32[1024,3]{0,1:T(4,128)S(1)} %bitcast.62), channel_id=1, replica_groups=mesh['ctx'=64,'head'=8] {'ctx'}, use_global_device_ids=true, to_apply=%region_5.6 | all-reduce | flops 3072 | bytes 24576 | tf_op jit(solution)/shard_map/pmax | solution.py:61
  637.5 1.0 copy.40
  638.6 0.0 reduce-scatter.9.cloned.1.call-update
  638.6 0.0 reduce-scatter.7.cloned.1.call-start
  638.7 1.7 copy.46
  640.4 0.0 copy-start.3
  640.4 0.1 bitcast_multiply_fusion
  640.6 0.0 copy-start.1
  640.6 1.6 copy.38
  642.2 0.0 reduce-scatter.7.cloned.1.call-update
  643.6 0.1 select_reduce_fusion
  643.7 193.9 %all_gather.11 = bf16[1024,384]{1,0:T(8,128)(2,1)S(1)} all-gather(bf16[16,384]{1,0:T(8,128)(2,1)S(1)} %copy-done.4), channel_id=1, replica_groups=mesh['ctx'=64,'head'=8] {'ctx'}, dimensions={0}, use_global_device_ids=true | all-gather | bytes 798720 | tf_op jit(solution)/shard_map/all_gather | solution.py:81
  837.6 1.0 broadcast_select_fusion
  838.6 198.3 %all_gather.10 = bf16[1024,384]{1,0:T(8,128)(2,1)S(1)} all-gather(bf16[16,384]{1,0:T(8,128)(2,1)S(1)} %copy-done.5), channel_id=1, replica_groups=mesh['ctx'=64,'head'=8] {'ctx'}, dimensions={0}, use_global_device_ids=true | all-gather | bytes 798720 | tf_op jit(solution)/shard_map/all_gather | solution.py:80
  1036.9 1.0 broadcast_select_fusion.1
  1037.8 68.1 %reduce-scatter.9.cloned.1.call-done = f32[16,3]{1,0:T(8,128)} async-done(((f32[1024,3]{1,0:T(8,128)}), f32[16,3]{1,0:T(8,128)}) %reduce-scatter.9.cloned.1.call-update) | async-done | bytes 208 | tf_op jit(solution)/shard_map/reduce_scatter | solution.py:69
  1106.0 872.8 %reduce-scatter.7.cloned.1.call-done = f32[16,384]{1,0:T(8,128)} async-done(((f32[1024,384]{1,0:T(8,128)}), f32[16,384]{1,0:T(8,128)}) %reduce-scatter.7.cloned.1.call-update) | async-done | bytes 24592 | tf_op jit(solution)/shard_map/reduce_scatter | solution.py:68
  1978.8 0.8 div.18
  1979.5 0.9 multiply_reduce_fusion
  1980.4 18.2 psum.7
  1998.7 1.4 multiply_convert_fusion
  (18 shorter events, 0.1 us)
Async XLA Ops:
  7.2 211.7 %copy-start.5 = (bf16[16,384]{1,0:T(8,128)(2,1)S(1)}, bf16[16,384]{1,0:T(8,128)(2,1)}, u32[]{:S(2)}) copy-start(bf16[16,384]{1,0:T(8,128)(2,1)} %param.13) | copy-start | bytes 36868
  7.2 1098.8 %reduce-scatter.9.cloned.1.call-start = ((), (), s32[]{:S(2)}) async-start(), calls=%async_computation.3 | async-start | bytes 532480 | tf_op jit(solution)/shard_map/reduce_scatter | solution.py:69
  218.7 3.7 copy-start
  218.8 3.7 copy-start.4
  221.6 3.2 copy-start.6
  638.6 1340.2 %reduce-scatter.7.cloned.1.call-start = ((), (), s32[]{:S(2)}) async-start(), calls=%async_computation.2 | async-start | bytes 1597440 | tf_op jit(solution)/shard_map/reduce_scatter | solution.py:68
  640.4 3.2 copy-start.3
  640.6 197.0 %copy-start.1 = (bf16[1024,384]{1,0:T(8,128)(2,1)S(1)}, bf16[1024,384]{1,0:T(8,128)(2,1)}, u32[]{:S(2)}) copy-start(bf16[1024,384]{1,0:T(8,128)(2,1)} %param.16) | copy-start | bytes 2359300
  642.2 394.7 %copy-start.2 = (bf16[1024,384]{1,0:T(8,128)(2,1)S(1)}, bf16[1024,384]{1,0:T(8,128)(2,1)}, u32[]{:S(2)}) copy-start(bf16[1024,384]{1,0:T(8,128)(2,1)} %param.15) | copy-start | bytes 2359300
Sparse Core Ops, SparseCore 0:
  638.7 467.2 reduce-scatter.8
  1113.5 865.1 reduce-scatter.6
where the time goes:
time: 2010 us
  blocking collectives  994 us (49%)
  waiting for transfers between devices  941 us (47%)
  local copies, waits for them, and re-layouts  41.4 us (2%)
    reduce_scatter x1, waiting for transfers between devices, body(): lax.psum_scatter(scaled_numer, 'ctx', scatter_dimension=0, tiled=True)  873 us
    pmax x1, blocking collectives, body(): row_max = lax.pmax(maxima, 'ctx')  374 us
    all_gather x1, blocking collectives, body(): queries = lax.all_gather(fresh_query, 'ctx', axis=0, tiled=True)  209 us
    all_gather x1, blocking collectives, body(): lax.all_gather(fresh_key, 'ctx', axis=0, tiled=True)  198 us
    all_gather x1, blocking collectives, body(): lax.all_gather(fresh_value, 'ctx', axis=0, tiled=True)  194 us
    reduce_scatter x1, waiting for transfers between devices, body(): lax.psum_scatter(scaled_denom, 'ctx', scatter_dimension=0, tiled=True)  68.1 us
  transfers between devices with their start and end apart: 2, of which 2 were waited for; matrix products, arithmetic and copies ran while one was open for 0% of the time, Pallas kernels for 0%

commit v1 on v0

v1 whole, which is shorter than its diff:
```python
import math

import jax
import jax.numpy as jnp
from jax import lax
from jax.experimental import pallas as pl
from jax.experimental.pallas import tpu as pltpu
from jax.sharding import Mesh, PartitionSpec as P

CTX = ("z", "x", "yh")
PLANE = ("x", "yh")
HEAD = ("yl", "core")
SPLIT = {"z": 8, "x": 4, "yh": 2, "yl": 4, "core": 2}
OWNERS = 64
ROWS = 16
HEADS = 3
DIM = 128
WIDTH = HEADS * DIM
TOKENS = OWNERS * ROWS
CACHE = 1024
BLOCK = 256
SENDERS = BLOCK // ROWS
MSG_ROWS = HEADS * ROWS + 8
FEATURES = 3072
LOG2E = math.log2(math.e)
SCALE2 = LOG2E / math.sqrt(DIM)
F32 = jnp.float32
BF16 = jnp.bfloat16


def dot_nt(a, b):
    return lax.dot_general(a, b, (((1,), (1,)), ((), ())), preferred_element_type=F32)


def softmax_part(query, key, value):
    scores = dot_nt(query, key)
    largest = jnp.max(scores, axis=1, keepdims=True)
    weights = jnp.exp2((scores - largest) * SCALE2).astype(BF16)
    with_ones = jnp.concatenate([value, jnp.ones_like(value)], axis=1)
    both = jnp.dot(weights, with_ones, preferred_element_type=F32)
    total = both[:, DIM:]
    return both[:, :DIM] / total, largest * SCALE2 + jnp.log2(total)


def attend_kernel(owner_ref, slope_ref, q_ref, k_ref, v_ref, slots_ref, msg_ref, nk_ref, nv_ref, sem):
    step = pl.program_id(0)
    copies = [
        pltpu.make_async_copy(k_ref, nk_ref, sem.at[0]),
        pltpu.make_async_copy(v_ref, nv_ref, sem.at[1]),
    ]

    @pl.when(step == 0)
    def _():
        for copy in copies:
            copy.start()

    slots = slots_ref[...]
    slot_ids = lax.broadcasted_iota(jnp.int32, slots.shape, 1)
    rank = jnp.sum(jnp.where(slots == owner_ref[0], slot_ids, 0).astype(F32), axis=1, keepdims=True)
    age = (rank + 1.0) / OWNERS
    lane = lax.broadcasted_iota(jnp.int32, (BLOCK, DIM), 1)
    piece = lane % 64
    stats = jnp.zeros((BLOCK, DIM), F32)
    for h in range(HEADS):
        cols = slice(h * DIM, (h + 1) * DIM)
        part, weight = softmax_part(q_ref[:, cols], k_ref[:, cols], v_ref[:, cols])
        weight = weight - age * (slope_ref[h] * LOG2E)
        msg_ref[:, h * ROWS : (h + 1) * ROWS, :] = part.astype(BF16).reshape(SENDERS, ROWS, DIM)
        for at in (0, 8, 16):
            rounded = weight.astype(BF16).astype(F32)
            stats = jnp.where(piece == at + h, rounded, stats)
            weight = weight - rounded
    halves = stats.reshape(SENDERS, 2, 8, DIM)
    first = lax.broadcasted_iota(jnp.int32, (SENDERS, 8, DIM), 2) < 64
    msg_ref[:, HEADS * ROWS :, :] = jnp.where(first, halves[:, 0], halves[:, 1]).astype(BF16)

    @pl.when(step == pl.num_programs(0) - 1)
    def _():
        for copy in copies:
            copy.wait()


def attend(owner, slope, query, key, value, slots):
    whole = lambda shape: pl.BlockSpec(shape, lambda i: (0,) * len(shape))
    return pl.pallas_call(
        attend_kernel,
        grid=(TOKENS // BLOCK,),
        in_specs=[
            pl.BlockSpec(memory_space=pltpu.SMEM),
            pl.BlockSpec(memory_space=pltpu.SMEM),
            pl.BlockSpec((BLOCK, WIDTH), lambda i: (i, 0)),
            whole((CACHE, WIDTH)),
            whole((CACHE, WIDTH)),
            whole((1, OWNERS)),
        ],
        out_specs=[
            pl.BlockSpec((SENDERS, MSG_ROWS, DIM), lambda i: (i, 0, 0)),
            pl.BlockSpec(memory_space=pl.ANY),
            pl.BlockSpec(memory_space=pl.ANY),
        ],
        out_shape=[
            jax.ShapeDtypeStruct((OWNERS, MSG_ROWS, DIM), BF16),
            jax.ShapeDtypeStruct((CACHE, WIDTH), BF16),
            jax.ShapeDtypeStruct((CACHE, WIDTH), BF16),
        ],
        scratch_shapes=[pltpu.SemaphoreType.DMA((2,))],
        compiler_params=pltpu.CompilerParams(vmem_limit_bytes=48 * 2**20),
        name="attend",
    )(owner, slope, query, key, value, slots)


def merge_kernel(owner_ref, evictor_ref, time_ref, q_ref, kv_ref, msg_ref, gate_ref, nk_in, nv_in, gated_ref, square_ref, nk_ref, nv_ref, sem):
    evicted = owner_ref[0] == evictor_ref[0]
    copies = [
        pltpu.make_async_copy(kv_ref.at[:, :WIDTH], nk_ref, sem.at[0]),
        pltpu.make_async_copy(kv_ref.at[:, WIDTH:], nv_ref, sem.at[1]),
    ]

    @pl.when(evicted)
    def _():
        for copy in copies:
            copy.start()

    lane = lax.broadcasted_iota(jnp.int32, (8, DIM), 1)
    fresh_parts = []
    fresh_weight = jnp.full((8, DIM), 0.0, F32)
    for h in range(HEADS):
        cols = slice(h * DIM, (h + 1) * DIM)
        vcols = slice(WIDTH + h * DIM, WIDTH + (h + 1) * DIM)
        part, weight = softmax_part(q_ref[:, cols], kv_ref[:, cols], kv_ref[:, vcols])
        fresh_parts.append(part)
        fresh_weight = jnp.where(lane == h, weight[:8], fresh_weight)
        fresh_weight = jnp.where(lane == 64 + h, weight[8:], fresh_weight)

    pieces = msg_ref[:, HEADS * ROWS :, :].astype(F32).reshape(OWNERS * 8, DIM)
    weights = pieces + pltpu.roll(pieces, DIM - 8, 1) + pltpu.roll(pieces, DIM - 16, 1)
    weights = weights.reshape(OWNERS, 8, DIM)
    largest = jnp.maximum(jnp.max(weights, axis=0), fresh_weight)
    factor = jnp.exp2(weights - largest[None])
    fresh_factor = jnp.exp2(fresh_weight - largest)
    total = jnp.sum(factor, axis=0) + fresh_factor
    squares = jnp.zeros((ROWS, 1), F32)
    picked = lax.broadcasted_iota(jnp.int32, (gate_ref.shape[0], DIM), 0) == time_ref[0]
    for h in range(HEADS):
        cols = slice(h * DIM, (h + 1) * DIM)
        parts = msg_ref[:, h * ROWS : (h + 1) * ROWS, :].astype(F32).reshape(OWNERS, 2, 8, DIM)
        halves = []
        for half in range(2):
            at = half * 64 + h
            summed = jnp.sum(factor[:, :, at : at + 1] * parts[:, half], axis=0)
            summed += fresh_factor[:, at : at + 1] * fresh_parts[h][half * 8 : half * 8 + 8]
            halves.append(summed / total[:, at : at + 1])
        attended = jnp.concatenate(halves, axis=0)
        squares += jnp.sum(attended * attended, axis=1, keepdims=True)
        gate = jnp.sum(jnp.where(picked, gate_ref[:, cols], 0.0), axis=0, keepdims=True)
        gated_ref[:, cols] = attended * gate
    row = lax.broadcasted_iota(jnp.int32, (ROWS, DIM), 0)
    column = lax.broadcasted_iota(jnp.int32, (ROWS, DIM), 1)
    line = jnp.sum(jnp.where(row == column, squares, 0.0), axis=0, keepdims=True)
    square_ref[...] = jnp.broadcast_to(line[None], square_ref.shape)

    @pl.when(evicted)
    def _():
        for copy in copies:
            copy.wait()


def merge(owner, evictor, timestep, query, kv, msg, gate, next_key, next_value):
    smem = pl.BlockSpec(memory_space=pltpu.SMEM)
    vmem = pl.BlockSpec(memory_space=pltpu.VMEM)
    hbm = pl.BlockSpec(memory_space=pl.ANY)
    return pl.pallas_call(
        merge_kernel,
        in_specs=[smem, smem, smem, vmem, vmem, vmem, vmem, hbm, hbm],
        out_specs=[vmem, vmem, hbm, hbm],
        out_shape=[
            jax.ShapeDtypeStruct((ROWS, WIDTH), F32),
            jax.ShapeDtypeStruct((8, 1, DIM), F32),
            jax.ShapeDtypeStruct((CACHE, WIDTH), BF16),
            jax.ShapeDtypeStruct((CACHE, WIDTH), BF16),
        ],
        input_output_aliases={7: 2, 8: 3},
        scratch_shapes=[pltpu.SemaphoreType.DMA((2,))],
        compiler_params=pltpu.CompilerParams(vmem_limit_bytes=48 * 2**20),
        name="merge",
    )(owner, evictor, timestep, query, kv, msg, gate, next_key, next_value)


def finish_kernel(gated_ref, square_ref, out_ref):
    line = jnp.sum(square_ref[...], axis=0)
    row = lax.broadcasted_iota(jnp.int32, (ROWS, DIM), 0)
    column = lax.broadcasted_iota(jnp.int32, (ROWS, DIM), 1)
    squares = jnp.sum(jnp.where(row == column, line, 0.0), axis=1, keepdims=True)
    out_ref[...] = (gated_ref[...] * lax.rsqrt(squares / FEATURES + 1e-06)).astype(BF16)


def spread(block, axis):
    copies = math.prod(SPLIT[name] for name in (axis if isinstance(axis, tuple) else (axis,)))
    sent = jnp.broadcast_to(block[None], (copies,) + block.shape)
    return lax.all_to_all(sent, axis, 0, 0, tiled=True)


def body(
    fresh_query,
    fresh_key,
    fresh_value,
    cache_key,
    cache_value,
    slot_owner,
    evictor,
    timestep,
    age_slope,
    time_gate,
):
    owner = lax.axis_index(CTX).astype(jnp.int32).reshape(1)
    fresh = jnp.concatenate([fresh_query, fresh_key, fresh_value], axis=1)
    plane = spread(fresh, PLANE).reshape(-1, 3 * WIDTH)
    kv = lax.all_gather(plane[:, WIDTH:], "z", axis=0, tiled=True)
    queries = spread(plane[:, :WIDTH], "z").reshape(TOKENS, WIDTH)
    msg, next_key, next_value = attend(
        owner, age_slope, queries, cache_key, cache_value, slot_owner.reshape(1, OWNERS)
    )
    msg = lax.all_to_all(msg, CTX, 0, 0, tiled=True)
    gated, squares, next_key, next_value = merge(
        owner, evictor, timestep, fresh_query, kv, msg, time_gate, next_key, next_value
    )
    squares = lax.all_to_all(squares, HEAD, 0, 0, tiled=True)
    attn_output = pl.pallas_call(
        finish_kernel,
        out_shape=jax.ShapeDtypeStruct((ROWS, WIDTH), BF16),
        name="finish",
    )(gated, squares)
    return attn_output, next_key, next_value


def solution(mesh):
    split = Mesh(mesh.devices.reshape(tuple(SPLIT.values())), tuple(SPLIT))
    both = P(CTX, HEAD)
    return jax.shard_map(
        body,
        mesh=split,
        in_specs=(both,) * 5 + (P(), P(), P(), P(HEAD), P(None, HEAD)),
        out_specs=(both, both, both),
        check_vma=False,
    )
```

time: 2010 us -> 127 us (0.06)
  blocking collectives: 994 us -> 34.4 us
  waiting for transfers between devices: 941 us -> 47 us
  local copies, waits for them, and re-layouts: 41.4 us -> 3.71 us
    reduce_scatter x2 -> x0, waiting for transfers between devices: 941 us -> none  [the longest x1 873 us: body(): lax.psum_scatter(scaled_numer, 'ctx', scatter_dimension=0, tiled=True)]
    all_gather x3 -> x0, blocking collectives: 601 us -> none  [the longest x1 209 us: body(): queries = lax.all_gather(fresh_query, 'ctx', axis=0, tiled=True)]
    pmax x1 -> x0, blocking collectives: 374 us -> none  [body(): row_max = lax.pmax(maxima, 'ctx')]
    all_to_all x0 -> x2, blocking collectives: none -> 34.4 us  [the longest x1 20.6 us: spread(): return lax.all_to_all(sent, axis, 0, 0, tiled=True)]
    dynamic_update_slice x6 -> x0, local copies, waits for them, and re-layouts: 31.3 us -> none  [body(): numerators, denominators, maxima = lax.map(weigh_block, query_blocks)]
    all_gather x0 -> x1, waiting for transfers between devices: none -> 23.8 us  [body(): kv = lax.all_gather(plane[:, WIDTH:], 'z', axis=0, tiled=True)]
    all_to_all x0 -> x2, waiting for transfers between devices: none -> 23.1 us  [the longest x1 20.5 us: spread(): return lax.all_to_all(sent, axis, 0, 0, tiled=True)]
  transfers between devices with their start and end apart: 2 -> 3, of which waited for: 2 -> 3; matrix products, arithmetic and copies ran while one was open for 0% -> 1% of each run, Pallas kernels for 0% -> 6%
where the time goes in v1:
time: 127 us; the launch traced here: 126 us
  waiting for transfers between devices  47 us (37%)
  blocking collectives  34.4 us (27%)
  between operations  15.4 us (12%)
  starting transfers between devices  14.7 us (12%)
  Pallas kernels  10.1 us (8%)
  local copies, waits for them, and re-layouts  3.71 us (3%)
    all_gather x1, waiting for transfers between devices, body(): kv = lax.all_gather(plane[:, WIDTH:], 'z', axis=0, tiled=True)  23.8 us
    all_to_all x1, blocking collectives, spread(): return lax.all_to_all(sent, axis, 0, 0, tiled=True)  20.6 us
    all_to_all x1, waiting for transfers between devices, spread(): return lax.all_to_all(sent, axis, 0, 0, tiled=True)  20.5 us
    all_to_all x1, blocking collectives, body(): squares = lax.all_to_all(squares, HEAD, 0, 0, tiled=True)  13.9 us
    all_to_all x1, starting transfers between devices, spread(): return lax.all_to_all(sent, axis, 0, 0, tiled=True)  10 us
    pallas_call x1, Pallas kernels, attend(): pl.pallas_call(attend_kernel, grid=(TOKENS // BLOCK,), in_specs=[pl.Block...  7.23 us
    all_to_all x1, starting transfers between devices, body(): msg = lax.all_to_all(msg, CTX, 0, 0, tiled=True)  4.66 us
    all_to_all x1, waiting for transfers between devices, body(): msg = lax.all_to_all(msg, CTX, 0, 0, tiled=True)  2.64 us
  transfers between devices with their start and end apart: 3, of which 3 were waited for; matrix products, arithmetic and copies ran while one was open for 1% of the time, Pallas kernels for 6%

profile of v1, /device:TPU:1, one launch (start us, length us, event | category | flops | bytes accessed | tf_op | source)
XLA Modules:
  0.0 126.1 jit_solution(12760201264478787756)
XLA Ops:
  7.2 0.7 pad_maximum_fusion
  7.9 20.6 %all_to_all.20 = bf16[8,16,1152]{2,1,0:T(8,128)(2,1)S(1)} all-to-all(bf16[8,16,1152]{2,1,0:T(8,128)(2,1)S(1)} %broadcast_in_dim.4), channel_id=1, replica_groups=mesh['z'=8,'x'=4,'yh'=2,'yl'=4,'core'=2] {'x','yh'}, dimensions={0} | all-to-all | bytes 589824 | tf_op jit(solution)/shard_map/all_to_all | solution.py:200
  28.5 0.0 copy-start.1
  28.5 0.0 copy-start.2
  28.5 0.0 copy-start.6
  28.5 0.0 copy-start.7
  28.6 1.0 broadcast_in_dim.5
  29.5 10.0 %all-to-all-start.1 = ((bf16[8,128,384]{2,1,0:T(8,128)(2,1)}), bf16[8,128,384]{2,1,0:T(8,128)(2,1)S(1)}, u32[]{:S(2)}, u32[]{:S(2)}) async-start(bf16[8,128,384]{2,1,0:T(8,128)(2,1)} %broadcast_in_dim.5), calls=%async_computation.1 | async-start | bytes 1572864 | tf_op jit(solution)/shard_map/all_to_all | solution.py:200
  39.5 0.0 all-gather.2.cloned.1.call-start
  39.6 0.7 slice.8
  40.3 0.0 all-gather.2.cloned.1.call-update
  40.3 20.5 %all-to-all-done.1 = bf16[8,128,384]{2,1,0:T(8,128)(2,1)S(1)} async-done(((bf16[8,128,384]{2,1,0:T(8,128)(2,1)}), bf16[8,128,384]{2,1,0:T(8,128)(2,1)S(1)}, u32[]{:S(2)}, u32[]{:S(2)}) %all-to-all-start.1) | async-done | bytes 786464 | tf_op jit(solution)/shard_map/all_to_all | solution.py:200
  60.8 0.0 copy-done.1
  60.8 0.0 copy-done.2
  60.8 0.0 copy-done.6
  60.8 0.0 copy-done.7
  60.8 0.0 copy-start.3
  60.8 0.0 copy-start.4
  60.8 7.2 %attend.1 = (bf16[64,56,128]{2,1,0:T(8,128)(2,1)}, bf16[1024,384]{1,0:T(8,128)(2,1)}, bf16[1024,384]{1,0:T(8,128)(2,1)}) custom-call(s32[1]{0:T(128)} %bitcast.owner_ref, f32[3]{0:T(128)S(1)} %copy-done.6, bf16[1024,384]{1,0:T(8,128)(2,1)S(1)} %bitcast.4, bf16[1024,384]{1,0:T(8,128)(2,1)S(1)} %copy-done.1, bf16[1024,384]{1,0:T(8,128)(2,1)S(1)} %copy-done.2, ...), custom_call_target="tpu_custom_call" | custom-call | tf_op jit(solution)/shard_map/attend/pallas_call | solution.py:85
  68.1 4.7 %all-to-all-start.2 = ((bf16[64,56,128]{2,1,0:T(8,128)(2,1)}), bf16[64,56,128]{2,1,0:T(8,128)(2,1)S(1)}, u32[]{:S(2)}, u32[]{:S(2)}) async-start(bf16[64,56,128]{2,1,0:T(8,128)(2,1)} %get-tuple-element.10), calls=%async_computation.2 | async-start | bytes 1835008 | tf_op jit(solution)/shard_map/all_to_all | solution.py:223
  74.0 23.8 %all-gather.2.cloned.1.call-done.kv_ref = bf16[1024,768]{1,0:T(8,128)(2,1)} async-done(((bf16[128,768]{1,0:T(8,128)(2,1)}), bf16[1024,768]{1,0:T(8,128)(2,1)}) %all-gather.2.cloned.1.call-update) | async-done | bytes 1572880 | tf_op jit(solution)/shard_map/all_gather | solution.py:218
  97.8 2.6 %all-to-all-done.2.msg_ref = bf16[64,56,128]{2,1,0:T(8,128)(2,1)S(1)} async-done(((bf16[64,56,128]{2,1,0:T(8,128)(2,1)}), bf16[64,56,128]{2,1,0:T(8,128)(2,1)S(1)}, u32[]{:S(2)}, u32[]{:S(2)}) %all-to-all-start.2) | async-done | bytes 917536 | tf_op jit(solution)/shard_map/all_to_all | solution.py:223
  100.5 0.0 copy-done.3
  100.5 0.0 copy-done.4
  100.5 0.0 copy-start
  100.5 1.4 %copy-done = bf16[1024,768]{1,0:T(8,128)(2,1)S(1)} copy-done((bf16[1024,768]{1,0:T(8,128)(2,1)S(1)}, bf16[1024,768]{1,0:T(8,128)(2,1)}, u32[]{:S(2)}) %copy-start) | copy-done | bytes 1572888
  101.9 1.5 %merge.1 = (f32[16,384]{1,0:T(8,128)S(1)}, f32[8,1,128]{2,1,0:T(1,128)S(1)}, bf16[1024,384]{1,0:T(8,128)(2,1)}, bf16[1024,384]{1,0:T(8,128)(2,1)}) custom-call(s32[1]{0:T(128)} %bitcast.owner_ref, s32[1]{0:T(128)S(6)} %copy.17.evictor_ref, s32[1]{0:T(128)S(6)} %copy.18.time_ref, ...), custom_call_target="tpu_custom_call", output_to_operand_aliasing={{2}: (7, {}), {3}: (8, {})} | custom-call | tf_op jit(solution)/shard_map/merge/pallas_call | solution.py:172
  103.4 0.0 copy-start.5
  103.4 0.6 copy-done.5
  104.0 13.9 %all_to_all.21.square_ref = f32[8,1,128]{2,1,0:T(1,128)} all-to-all(f32[8,1,128]{2,1,0:T(1,128)S(1)} %get-tuple-element.14), channel_id=1, replica_groups=mesh['z'=8,'x'=4,'yh'=2,'yl'=4,'core'=2] {'yl','core'}, dimensions={0} | all-to-all | bytes 8192 | tf_op jit(solution)/shard_map/all_to_all | solution.py:227
  117.9 1.4 %finish.1 = bf16[16,384]{1,0:T(8,128)(2,1)} custom-call(f32[16,384]{1,0:T(8,128)} %copy-done.5, f32[8,1,128]{2,1,0:T(1,128)} %all_to_all.21.square_ref), custom_call_target="tpu_custom_call" | custom-call | tf_op jit(solution)/shard_map/finish/pallas_call | solution.py:228
  (2 shorter events, 0.0 us)
Async XLA Ops:
  28.5 32.3 %copy-start.1 = (bf16[1024,384]{1,0:T(8,128)(2,1)S(1)}, bf16[1024,384]{1,0:T(8,128)(2,1)}, u32[]{:S(2)}) copy-start(bf16[1024,384]{1,0:T(8,128)(2,1)} %k_ref.1) | copy-start | bytes 2359300
  28.5 32.3 %copy-start.2 = (bf16[1024,384]{1,0:T(8,128)(2,1)S(1)}, bf16[1024,384]{1,0:T(8,128)(2,1)}, u32[]{:S(2)}) copy-start(bf16[1024,384]{1,0:T(8,128)(2,1)} %v_ref.1) | copy-start | bytes 2359300
  28.5 32.3 %copy-start.6 = (f32[3]{0:T(128)S(1)}, f32[3]{0:T(128)}, u32[]{:S(2)}) copy-start(f32[3]{0:T(128)} %slope_ref.1) | copy-start | bytes 40
  28.5 32.3 %copy-start.7 = (s32[64]{0:T(128)S(1)}, s32[64]{0:T(128)}, u32[]{:S(2)}) copy-start(s32[64]{0:T(128)} %param.15) | copy-start | bytes 772
  29.5 31.3 %all-to-all-start.1 = ((bf16[8,128,384]{2,1,0:T(8,128)(2,1)}), bf16[8,128,384]{2,1,0:T(8,128)(2,1)S(1)}, u32[]{:S(2)}, u32[]{:S(2)}) async-start(bf16[8,128,384]{2,1,0:T(8,128)(2,1)} %broadcast_in_dim.5), calls=%async_computation.1 | async-start | bytes 1572864 | tf_op jit(solution)/shard_map/all_to_all | solution.py:200
  39.5 58.3 %all-gather.2.cloned.1.call-start = ((), (), s32[]{:S(2)}) async-start(), calls=%async_computation.4 | async-start | bytes 1769472 | tf_op jit(solution)/shard_map/all_gather | solution.py:218
  60.8 39.7 %copy-start.3 = (f32[50,384]{1,0:T(8,128)S(1)}, f32[50,384]{1,0:T(8,128)}, u32[]{:S(2)}) copy-start(f32[50,384]{1,0:T(8,128)} %gate_ref.1) | copy-start | bytes 230404
  60.8 39.7 %copy-start.4 = (bf16[16,384]{1,0:T(8,128)(2,1)S(1)}, bf16[16,384]{1,0:T(8,128)(2,1)}, u32[]{:S(2)}) copy-start(bf16[16,384]{1,0:T(8,128)(2,1)} %q_ref.1) | copy-start | bytes 36868
  68.1 32.4 %all-to-all-start.2 = ((bf16[64,56,128]{2,1,0:T(8,128)(2,1)}), bf16[64,56,128]{2,1,0:T(8,128)(2,1)S(1)}, u32[]{:S(2)}, u32[]{:S(2)}) async-start(bf16[64,56,128]{2,1,0:T(8,128)(2,1)} %get-tuple-element.10), calls=%async_computation.2 | async-start | bytes 1835008 | tf_op jit(solution)/shard_map/all_to_all | solution.py:223
  100.5 1.4 %copy-start = (bf16[1024,768]{1,0:T(8,128)(2,1)S(1)}, bf16[1024,768]{1,0:T(8,128)(2,1)}, u32[]{:S(2)}) copy-start(bf16[1024,768]{1,0:T(8,128)(2,1)} %all-gather.2.cloned.1.call-done.kv_ref) | copy-start | bytes 4718596
  103.4 0.6 copy-start.5
Sparse Core Ops, SparseCore 0:
  42.5 55.3 all-gather.1

commit v2 on v1

v2 whole, which is shorter than its diff:
```python
import math

import jax
import jax.numpy as jnp
from jax import lax
from jax.experimental import pallas as pl
from jax.experimental.pallas import tpu as pltpu
from jax.sharding import Mesh, PartitionSpec as P

CTX = ("z", "x", "yh")
SHEET = ("z", "yh")
HEAD = ("yl", "core")
SPLIT = {"z": 8, "x": 4, "yh": 2, "yl": 4, "core": 2}
OWNERS = 64
ROWS = 16
HEADS = 3
DIM = 128
WIDTH = HEADS * DIM
TOKENS = OWNERS * ROWS
CACHE = 1024
BLOCK = 1024
SENDERS = BLOCK // ROWS
MSG_ROWS = HEADS * ROWS + 8
FEATURES = 3072
TOP = 32000.0
LOG2E = math.log2(math.e)
SCALE2 = LOG2E / math.sqrt(DIM)
F32 = jnp.float32
BF16 = jnp.bfloat16
I16 = jnp.int16
I32 = jnp.int32


def dot_nt(a, b):
    return lax.dot_general(a, b, (((1,), (1,)), ((), ())), preferred_element_type=F32)


def with_ones(value):
    return jnp.concatenate([value, jnp.ones_like(value)], axis=1)


def softmax_part(query, key, value, fresh_key, fresh_value, penalty):
    cached = dot_nt(query, key)
    fresh = dot_nt(query, fresh_key)
    largest = jnp.maximum(
        jnp.max(cached, axis=1, keepdims=True) * SCALE2 - penalty,
        jnp.max(fresh, axis=1, keepdims=True) * SCALE2,
    )
    cached_weights = jnp.exp2(cached * SCALE2 - (largest + penalty)).astype(BF16)
    fresh_weights = jnp.exp2(fresh * SCALE2 - largest).astype(BF16)
    both = jnp.dot(cached_weights, with_ones(value), preferred_element_type=F32)
    both += jnp.dot(fresh_weights, with_ones(fresh_value), preferred_element_type=F32)
    total = both[:, DIM:]
    return both[:, :DIM] / total, largest + jnp.log2(total)


def attend_kernel(owner_ref, slope_ref, q_ref, k_ref, v_ref, fk_ref, fv_ref, slots_ref, msg_ref, nk_ref, nv_ref, sem):
    step = pl.program_id(0)
    copies = [
        pltpu.make_async_copy(k_ref, nk_ref, sem.at[0]),
        pltpu.make_async_copy(v_ref, nv_ref, sem.at[1]),
    ]

    @pl.when(step == 0)
    def _():
        for copy in copies:
            copy.start()

    slots = slots_ref[...]
    slot_ids = lax.broadcasted_iota(I32, slots.shape, 1)
    rank = jnp.sum(jnp.where(slots == owner_ref[0], slot_ids, 0).astype(F32), axis=1, keepdims=True)
    age = (rank + 1.0) / OWNERS
    piece = lax.broadcasted_iota(I32, (BLOCK, DIM), 1) % 64
    stats = jnp.zeros((BLOCK, DIM), I32)
    for h in range(HEADS):
        cols = slice(h * DIM, (h + 1) * DIM)
        part, weight = softmax_part(
            q_ref[:, cols],
            k_ref[:, cols],
            v_ref[:, cols],
            fk_ref[:, cols],
            fv_ref[:, cols],
            age * (slope_ref[h] * LOG2E),
        )
        reach = jnp.max(jnp.abs(part), axis=1, keepdims=True)
        power = jnp.floor(jnp.log2(jnp.maximum(reach, 1e-30))) + 1.0
        codes = jnp.round(part * (jnp.exp2(-power) * TOP)).astype(I32)
        msg_ref[:, h * ROWS : (h + 1) * ROWS, :] = codes.astype(I16).reshape(SENDERS, ROWS, DIM)
        fixed = jnp.round(weight * 65536.0).astype(I32)
        high = (fixed + 32768) >> 16
        low = fixed - (high << 16)
        stats = jnp.where(piece == h, high, stats)
        stats = jnp.where(piece == 8 + h, low, stats)
        stats = jnp.where(piece == 16 + h, power.astype(I32), stats)
    halves = stats.reshape(SENDERS, 2, 8, DIM)
    early = lax.broadcasted_iota(I32, (SENDERS, 8, DIM), 2) < 64
    packed = jnp.where(early, halves[:, 0], halves[:, 1])
    msg_ref[:, HEADS * ROWS :, :] = packed.astype(I16)

    @pl.when(step == pl.num_programs(0) - 1)
    def _():
        for copy in copies:
            copy.wait()


def attend(owner, slope, query, key, value, fresh_key, fresh_value, slots):
    smem = pl.BlockSpec(memory_space=pltpu.SMEM)
    hbm = pl.BlockSpec(memory_space=pl.ANY)
    whole = lambda shape: pl.BlockSpec(shape, lambda i: (0,) * len(shape))
    pairs = TOKENS * (CACHE + ROWS) * HEADS
    return pl.pallas_call(
        attend_kernel,
        grid=(TOKENS // BLOCK,),
        in_specs=[
            smem,
            smem,
            pl.BlockSpec((BLOCK, WIDTH), lambda i: (i, 0)),
            whole((CACHE, WIDTH)),
            whole((CACHE, WIDTH)),
            whole((ROWS, WIDTH)),
            whole((ROWS, WIDTH)),
            whole((1, OWNERS)),
        ],
        out_specs=[pl.BlockSpec((SENDERS, MSG_ROWS, DIM), lambda i: (i, 0, 0)), hbm, hbm],
        out_shape=[jax.ShapeDtypeStruct((OWNERS, MSG_ROWS, DIM), I16)]
        + [jax.ShapeDtypeStruct((CACHE, WIDTH), BF16)] * 2,
        scratch_shapes=[pltpu.SemaphoreType.DMA((2,))],
        cost_estimate=pl.CostEstimate(
            flops=6 * DIM * pairs, bytes_accessed=4 * CACHE * WIDTH, transcendentals=pairs
        ),
        compiler_params=pltpu.CompilerParams(vmem_limit_bytes=40 * 2**20),
        name="attend",
    )(owner, slope, query, key, value, fresh_key, fresh_value, slots)


def merge_kernel(time_ref, msg_ref, gate_ref, gated_ref, square_ref):
    stats = msg_ref[:, HEADS * ROWS :, :].astype(I32).astype(F32).reshape(OWNERS * 8, DIM)
    weights = stats + pltpu.roll(stats, DIM - 8, 1) * (1.0 / 65536.0)
    powers = pltpu.roll(stats, DIM - 16, 1).reshape(OWNERS, 8, DIM)
    weights = weights.reshape(OWNERS, 8, DIM)
    largest = jnp.max(weights, axis=0)
    factor = jnp.exp2(weights - largest[None])
    total = jnp.sum(factor, axis=0)
    factor = factor * jnp.exp2(powers)
    squares = jnp.zeros((ROWS, 1), F32)
    picked = lax.broadcasted_iota(I32, (gate_ref.shape[0], DIM), 0) == time_ref[0]
    for h in range(HEADS):
        cols = slice(h * DIM, (h + 1) * DIM)
        codes = msg_ref[:, h * ROWS : (h + 1) * ROWS, :]
        parts = codes.astype(I32).astype(F32).reshape(OWNERS, 2, 8, DIM)
        halves = []
        for half in range(2):
            at = half * 64 + h
            summed = jnp.sum(factor[:, :, at : at + 1] * parts[:, half], axis=0)
            halves.append(summed / (total[:, at : at + 1] * TOP))
        attended = jnp.concatenate(halves, axis=0)
        squares += jnp.sum(attended * attended, axis=1, keepdims=True)
        gate = jnp.sum(jnp.where(picked, gate_ref[:, cols], 0.0), axis=0, keepdims=True)
        gated_ref[:, cols] = attended * gate
    row = lax.broadcasted_iota(I32, (ROWS, DIM), 0)
    column = lax.broadcasted_iota(I32, (ROWS, DIM), 1)
    line = jnp.sum(jnp.where(row == column, squares, 0.0), axis=0, keepdims=True)
    square_ref[...] = jnp.broadcast_to(line[None], square_ref.shape)


def merge(timestep, msg, gate):
    smem = pl.BlockSpec(memory_space=pltpu.SMEM)
    vmem = pl.BlockSpec(memory_space=pltpu.VMEM)
    return pl.pallas_call(
        merge_kernel,
        in_specs=[smem, vmem, vmem],
        out_specs=[vmem, vmem],
        out_shape=[
            jax.ShapeDtypeStruct((ROWS, WIDTH), F32),
            jax.ShapeDtypeStruct((8, 1, DIM), F32),
        ],
        compiler_params=pltpu.CompilerParams(vmem_limit_bytes=40 * 2**20),
        name="merge",
    )(timestep, msg, gate)


def evict_kernel(owner_ref, evictor_ref, kv_ref, nk_in, nv_in, nk_ref, nv_ref, held, sem):
    @pl.when(owner_ref[0] == evictor_ref[0])
    def _():
        fetch = pltpu.make_async_copy(kv_ref, held, sem.at[0])
        fetch.start()
        fetch.wait()
        copies = []
        for x in range(SPLIT["x"]):
            for half, out_ref in enumerate((nk_ref, nv_ref)):
                copies.append(
                    pltpu.make_async_copy(
                        held.at[x, :, :, half * WIDTH : (half + 1) * WIDTH],
                        out_ref.at[:, x],
                        sem.at[1 + 2 * x + half],
                    )
                )
        for copy in copies:
            copy.start()
        for copy in copies:
            copy.wait()


def evict(owner, evictor, kv, next_key, next_value):
    smem = pl.BlockSpec(memory_space=pltpu.SMEM)
    hbm = pl.BlockSpec(memory_space=pl.ANY)
    rows = SPLIT["yh"] * ROWS
    gathered = (SPLIT["x"], SPLIT["z"], rows, 2 * WIDTH)
    cached = (SPLIT["z"], SPLIT["x"], rows, WIDTH)
    shape = jax.ShapeDtypeStruct(cached, BF16)
    outs = pl.pallas_call(
        evict_kernel,
        in_specs=[smem, smem, hbm, hbm, hbm],
        out_specs=[hbm, hbm],
        out_shape=[shape, shape],
        input_output_aliases={3: 0, 4: 1},
        scratch_shapes=[
            pltpu.VMEM(gathered, BF16),
            pltpu.SemaphoreType.DMA((1 + 2 * SPLIT["x"],)),
        ],
        compiler_params=pltpu.CompilerParams(vmem_limit_bytes=60 * 2**20),
        name="evict",
    )(owner, evictor, kv.reshape(gathered), next_key.reshape(cached), next_value.reshape(cached))
    return [out.reshape(CACHE, WIDTH) for out in outs]


def spread(block, axis):
    copies = math.prod(SPLIT[name] for name in (axis if isinstance(axis, tuple) else (axis,)))
    sent = jnp.broadcast_to(block[None], (copies,) + block.shape)
    return lax.all_to_all(sent, axis, 0, 0, tiled=True)


def body(
    fresh_query,
    fresh_key,
    fresh_value,
    cache_key,
    cache_value,
    slot_owner,
    evictor,
    timestep,
    age_slope,
    time_gate,
):
    owner = lax.axis_index(CTX).astype(I32).reshape(1)
    fresh = jnp.concatenate([fresh_query, fresh_key, fresh_value], axis=1)
    sheet = spread(fresh, SHEET).reshape(-1, 3 * WIDTH)
    kv = lax.all_gather(sheet[:, WIDTH:], "x", axis=0, tiled=True)
    queries = spread(sheet[:, :WIDTH], "x").reshape(TOKENS, WIDTH)
    msg, next_key, next_value = attend(
        owner, age_slope, queries, cache_key, cache_value, fresh_key, fresh_value, slot_owner.reshape(1, OWNERS)
    )
    msg = lax.all_to_all(msg, ("x",) + SHEET, 0, 0, tiled=True)
    gated, squares = merge(timestep, msg, time_gate)
    squares = lax.all_to_all(squares, HEAD, 0, 0, tiled=True)
    next_key, next_value = evict(owner, evictor, kv, next_key, next_value)
    squares = jnp.sum(squares, axis=(0, 1))[:ROWS, None]
    attn_output = (gated * lax.rsqrt(squares / FEATURES + 1e-06)).astype(BF16)
    return attn_output, next_key, next_value


def solution(mesh):
    split = Mesh(mesh.devices.reshape(tuple(SPLIT.values())), tuple(SPLIT))
    both = P(CTX, HEAD)
    return jax.shard_map(
        body,
        mesh=split,
        in_specs=(both,) * 5 + (P(), P(), P(), P(HEAD), P(None, HEAD)),
        out_specs=(both, both, both),
        check_vma=False,
    )
```

time: 127 us -> 125 us (0.984)
  starting transfers between devices: 14.7 us -> 25.7 us
  waiting for transfers between devices: 47 us -> 36 us
  local copies, waits for them, and re-layouts: 3.71 us -> 1.84 us
    all_to_all x1 -> x2, waiting for transfers between devices: 2.64 us -> 27.3 us  [the longest x1 23.3 us: body(): msg = lax.all_to_all(msg, ('x',) + SHEET, 0, 0, tiled=True)]
    all_gather x1, waiting for transfers between devices: 23.8 us -> 0.02 us  [body(): kv = lax.all_gather(sheet[:, WIDTH:], 'x', axis=0, tiled=True)]
    all_to_all x1 -> x2, starting transfers between devices: 4.66 us -> 21.6 us  [the longest x1 11.2 us: body(): msg = lax.all_to_all(msg, ('x',) + SHEET, 0, 0, tiled=True)]
    all_to_all x1 -> x0, blocking collectives: 13.9 us -> none  [body(): squares = lax.all_to_all(squares, HEAD, 0, 0, tiled=True)]
    all_to_all x1, blocking collectives: 20.6 us -> 33.9 us  [spread(): return lax.all_to_all(sent, axis, 0, 0, tiled=True)]
    all_to_all x1, waiting for transfers between devices: 20.5 us -> 8.7 us  [spread(): return lax.all_to_all(sent, axis, 0, 0, tiled=True)]
    all_to_all x1, starting transfers between devices: 10 us -> 4.16 us  [spread(): return lax.all_to_all(sent, axis, 0, 0, tiled=True)]
    unnamed x16 -> x14, local copies, waits for them, and re-layouts: 2.04 us -> 0.03 us
  transfers between devices with their start and end apart: 3 -> 4, of which waited for: 3 -> 3; matrix products, arithmetic and copies ran while one was open for 1% -> 1% of each run, Pallas kernels for 6% -> 8%
where the time goes in v2:
time: 125 us; the launch traced here: 124 us
  waiting for transfers between devices  36 us (29%)
  blocking collectives  33.9 us (27%)
  starting transfers between devices  25.7 us (21%)
  between operations  15.4 us (12%)
  Pallas kernels  9.63 us (8%)
  local copies, waits for them, and re-layouts  1.84 us (1%)
  other arithmetic  1.46 us (1%)
    all_to_all x1, blocking collectives, spread(): return lax.all_to_all(sent, axis, 0, 0, tiled=True)  33.9 us
    all_to_all x1, waiting for transfers between devices, body(): msg = lax.all_to_all(msg, ('x',) + SHEET, 0, 0, tiled=True)  23.3 us
    all_to_all x1, starting transfers between devices, body(): msg = lax.all_to_all(msg, ('x',) + SHEET, 0, 0, tiled=True)  11.2 us
    all_to_all x1, starting transfers between devices, body(): squares = lax.all_to_all(squares, HEAD, 0, 0, tiled=True)  10.3 us
    all_to_all x1, waiting for transfers between devices, spread(): return lax.all_to_all(sent, axis, 0, 0, tiled=True)  8.7 us
    pallas_call x1, Pallas kernels, attend(): pl.pallas_call(attend_kernel, grid=(TOKENS // BLOCK,), in_specs=[smem, sm...  8 us
    all_to_all x1, starting transfers between devices, spread(): return lax.all_to_all(sent, axis, 0, 0, tiled=True)  4.16 us
    all_to_all x1, waiting for transfers between devices, body(): squares = lax.all_to_all(squares, HEAD, 0, 0, tiled=True)  3.97 us
  transfers between devices with their start and end apart: 4, of which 3 were waited for; matrix products, arithmetic and copies ran while one was open for 1% of the time, Pallas kernels for 8%

profile of v2, /device:TPU:1, one launch (start us, length us, event | category | flops | bytes accessed | tf_op | source)
XLA Modules:
  0.0 124.1 jit_solution(10611863619428994531)
XLA Ops:
  7.2 0.7 pad_maximum_fusion
  8.0 33.9 %all_to_all.20 = bf16[16,16,1152]{2,1,0:T(8,128)(2,1)S(1)} all-to-all(bf16[16,16,1152]{2,1,0:T(8,128)(2,1)S(1)} %broadcast_in_dim.4), channel_id=1, replica_groups=mesh['z'=8,'x'=4,'yh'=2,'yl'=4,'core'=2] {'z','yh'}, dimensions={0} | all-to-all | bytes 1179648 | tf_op jit(solution)/shard_map/all_to_all | solution.py:230
  41.9 0.9 broadcast_in_dim.5
  42.9 0.0 copy-start.1
  42.9 0.0 copy-start.2
  42.9 0.0 copy-start.3
  42.9 0.0 copy-start.4
  42.9 0.0 copy-start.5
  42.9 0.0 copy-start.6
  42.9 4.2 %all-to-all-start.1 = ((bf16[4,256,384]{2,1,0:T(8,128)(2,1)}), bf16[4,256,384]{2,1,0:T(8,128)(2,1)S(1)}, u32[]{:S(2)}, u32[]{:S(2)}) async-start(bf16[4,256,384]{2,1,0:T(8,128)(2,1)} %broadcast_in_dim.5), calls=%async_computation.1 | async-start | bytes 1572864 | tf_op jit(solution)/shard_map/all_to_all | solution.py:230
  47.1 0.0 all-gather.2.cloned.1.call-start
  47.1 0.8 slice.13
  47.9 0.0 all-gather.2.cloned.1.call-update
  47.9 8.7 %all-to-all-done.1 = bf16[4,256,384]{2,1,0:T(8,128)(2,1)S(1)} async-done(((bf16[4,256,384]{2,1,0:T(8,128)(2,1)}), bf16[4,256,384]{2,1,0:T(8,128)(2,1)S(1)}, u32[]{:S(2)}, u32[]{:S(2)}) %all-to-all-start.1) | async-done | bytes 786464 | tf_op jit(solution)/shard_map/all_to_all | solution.py:230
  56.6 0.0 copy-done.1
  56.6 0.0 copy-done.2
  56.6 0.0 copy-done.3
  56.6 0.0 copy-done.4
  56.6 0.0 copy-done.5
  56.6 0.0 copy-done.6
  56.6 8.0 %attend.1 = (s16[64,56,128]{2,1,0:T(8,128)(2,1)}, bf16[1024,384]{1,0:T(8,128)(2,1)}, bf16[1024,384]{1,0:T(8,128)(2,1)}) custom-call(s32[1]{0:T(128)} %bitcast.owner_ref, f32[3]{0:T(128)S(1)} %copy-done.5, bf16[1024,384]{1,0:T(8,128)(2,1)S(1)} %bitcast.9, bf16[1024,384]{1,0:T(8,128)(2,1)S(1)} %copy-done.3, bf16[1024,384]{1,0:T(8,128)(2,1)S(1)} %copy-done.4, ...), custom_call_target="tpu_custom_call" | custom-call | flops 2453667840 | bytes 1572864 | tf_op jit(solution)/shard_map/attend/pallas_call | solution.py:111
  64.6 0.0 copy-start
  64.6 11.2 %all-to-all-start.2 = ((s16[64,56,128]{2,1,0:T(8,128)(2,1)}), s16[64,56,128]{2,1,0:T(8,128)(2,1)S(1)}, u32[]{:S(2)}, u32[]{:S(2)}) async-start(s16[64,56,128]{2,1,0:T(8,128)(2,1)} %get-tuple-element.10), calls=%async_computation.2 | async-start | bytes 1835008 | tf_op jit(solution)/shard_map/all_to_all | solution.py:253
  76.5 23.3 %all-to-all-done.2.msg_ref = s16[64,56,128]{2,1,0:T(8,128)(2,1)S(1)} async-done(((s16[64,56,128]{2,1,0:T(8,128)(2,1)}), s16[64,56,128]{2,1,0:T(8,128)(2,1)S(1)}, u32[]{:S(2)}, u32[]{:S(2)}) %all-to-all-start.2) | async-done | bytes 917536 | tf_op jit(solution)/shard_map/all_to_all | solution.py:253
  99.9 0.0 copy-done
  99.9 1.5 %merge.1 = (f32[16,384]{1,0:T(8,128)S(1)}, f32[8,1,128]{2,1,0:T(1,128)}) custom-call(s32[1]{0:T(128)S(6)} %copy.18.time_ref, s16[64,56,128]{2,1,0:T(8,128)(2,1)S(1)} %all-to-all-done.2.msg_ref, f32[50,384]{1,0:T(8,128)S(1)} %copy-done), custom_call_target="tpu_custom_call" | custom-call | tf_op jit(solution)/shard_map/merge/pallas_call | solution.py:169
  101.4 10.3 %all-to-all-start.3 = ((f32[8,1,128]{2,1,0:T(1,128)}), f32[8,1,128]{2,1,0:T(1,128)S(1)}, u32[]{:S(2)}, u32[]{:S(2)}) async-start(f32[8,1,128]{2,1,0:T(1,128)} %get-tuple-element.12), calls=%async_computation.3 | async-start | bytes 8192 | tf_op jit(solution)/shard_map/all_to_all | solution.py:255
  112.4 0.0 all-gather.2.cloned.1.call-done
  112.4 0.1 evict.1
  112.5 4.0 %all-to-all-done.3 = f32[8,1,128]{2,1,0:T(1,128)S(1)} async-done(((f32[8,1,128]{2,1,0:T(1,128)}), f32[8,1,128]{2,1,0:T(1,128)S(1)}, u32[]{:S(2)}, u32[]{:S(2)}) %all-to-all-start.3) | async-done | bytes 4128 | tf_op jit(solution)/shard_map/all_to_all | solution.py:255
  116.5 0.7 multiply_convert_fusion
  (4 shorter events, 0.1 us)
Async XLA Ops:
  42.9 13.7 %copy-start.1 = (bf16[16,384]{1,0:T(8,128)(2,1)S(1)}, bf16[16,384]{1,0:T(8,128)(2,1)}, u32[]{:S(2)}) copy-start(bf16[16,384]{1,0:T(8,128)(2,1)} %fv_ref.1) | copy-start | bytes 36868
  42.9 13.7 %copy-start.2 = (bf16[16,384]{1,0:T(8,128)(2,1)S(1)}, bf16[16,384]{1,0:T(8,128)(2,1)}, u32[]{:S(2)}) copy-start(bf16[16,384]{1,0:T(8,128)(2,1)} %fk_ref.1) | copy-start | bytes 36868
  42.9 13.7 %copy-start.3 = (bf16[1024,384]{1,0:T(8,128)(2,1)S(1)}, bf16[1024,384]{1,0:T(8,128)(2,1)}, u32[]{:S(2)}) copy-start(bf16[1024,384]{1,0:T(8,128)(2,1)} %k_ref.1) | copy-start | bytes 2359300
  42.9 13.7 %copy-start.4 = (bf16[1024,384]{1,0:T(8,128)(2,1)S(1)}, bf16[1024,384]{1,0:T(8,128)(2,1)}, u32[]{:S(2)}) copy-start(bf16[1024,384]{1,0:T(8,128)(2,1)} %v_ref.1) | copy-start | bytes 2359300
  42.9 13.7 %copy-start.5 = (f32[3]{0:T(128)S(1)}, f32[3]{0:T(128)}, u32[]{:S(2)}) copy-start(f32[3]{0:T(128)} %slope_ref.1) | copy-start | bytes 40
  42.9 13.7 %copy-start.6 = (s32[64]{0:T(128)S(1)}, s32[64]{0:T(128)}, u32[]{:S(2)}) copy-start(s32[64]{0:T(128)} %param.15) | copy-start | bytes 772
  42.9 13.7 %all-to-all-start.1 = ((bf16[4,256,384]{2,1,0:T(8,128)(2,1)}), bf16[4,256,384]{2,1,0:T(8,128)(2,1)S(1)}, u32[]{:S(2)}, u32[]{:S(2)}) async-start(bf16[4,256,384]{2,1,0:T(8,128)(2,1)} %broadcast_in_dim.5), calls=%async_computation.1 | async-start | bytes 1572864 | tf_op jit(solution)/shard_map/all_to_all | solution.py:230
  47.1 65.3 %all-gather.2.cloned.1.call-start = ((), (), s32[]{:S(2)}) async-start(), calls=%async_computation.4 | async-start | bytes 1966080 | tf_op jit(solution)/shard_map/all_gather | solution.py:248
  64.6 35.2 %copy-start = (f32[50,384]{1,0:T(8,128)S(1)}, f32[50,384]{1,0:T(8,128)}, u32[]{:S(2)}) copy-start(f32[50,384]{1,0:T(8,128)} %gate_ref.1) | copy-start | bytes 230404
  64.6 35.2 %all-to-all-start.2 = ((s16[64,56,128]{2,1,0:T(8,128)(2,1)}), s16[64,56,128]{2,1,0:T(8,128)(2,1)S(1)}, u32[]{:S(2)}, u32[]{:S(2)}) async-start(s16[64,56,128]{2,1,0:T(8,128)(2,1)} %get-tuple-element.10), calls=%async_computation.2 | async-start | bytes 1835008 | tf_op jit(solution)/shard_map/all_to_all | solution.py:253
  101.4 15.1 %all-to-all-start.3 = ((f32[8,1,128]{2,1,0:T(1,128)}), f32[8,1,128]{2,1,0:T(1,128)S(1)}, u32[]{:S(2)}, u32[]{:S(2)}) async-start(f32[8,1,128]{2,1,0:T(1,128)} %get-tuple-element.12), calls=%async_computation.3 | async-start | bytes 8192 | tf_op jit(solution)/shard_map/all_to_all | solution.py:255
Sparse Core Ops, SparseCore 0:
  50.0 34.8 all-gather.1

commit v3 on v2

--- a/solution.py
+++ b/solution.py
@@ -20,6 +20,7 @@
 CACHE = 1024
 BLOCK = 1024
 SENDERS = BLOCK // ROWS
+TURNS = (0, 1, 3, 2)
 MSG_ROWS = HEADS * ROWS + 8
 FEATURES = 3072
 TOP = 32000.0
@@ -179,20 +180,27 @@
     )(timestep, msg, gate)
 
 
-def evict_kernel(owner_ref, evictor_ref, kv_ref, nk_in, nv_in, nk_ref, nv_ref, held, sem):
+def evict_kernel(owner_ref, evictor_ref, *refs):
+    blocks, (nk_ref, nv_ref, held, sem) = refs[: len(TURNS)], refs[-4:]
+
     @pl.when(owner_ref[0] == evictor_ref[0])
     def _():
-        fetch = pltpu.make_async_copy(kv_ref, held, sem.at[0])
-        fetch.start()
-        fetch.wait()
+        fetches = [
+            pltpu.make_async_copy(block, held.at[at], sem.at[at]) for at, block in enumerate(blocks)
+        ]
+        for fetch in fetches:
+            fetch.start()
+        for fetch in fetches:
+            fetch.wait()
         copies = []
-        for x in range(SPLIT["x"]):
+        for at, turn in enumerate(TURNS):
+            x = ((owner_ref[0] >> 1) & 3) ^ turn
             for half, out_ref in enumerate((nk_ref, nv_ref)):
                 copies.append(
                     pltpu.make_async_copy(
-                        held.at[x, :, :, half * WIDTH : (half + 1) * WIDTH],
+                        held.at[at, :, :, half * WIDTH : (half + 1) * WIDTH],
                         out_ref.at[:, x],
-                        sem.at[1 + 2 * x + half],
+                        sem.at[len(TURNS) + 2 * at + half],
                     )
                 )
         for copy in copies:
@@ -201,27 +209,49 @@
             copy.wait()
 
 
-def evict(owner, evictor, kv, next_key, next_value):
+def evict(owner, evictor, blocks, next_key, next_value):
     smem = pl.BlockSpec(memory_space=pltpu.SMEM)
     hbm = pl.BlockSpec(memory_space=pl.ANY)
     rows = SPLIT["yh"] * ROWS
-    gathered = (SPLIT["x"], SPLIT["z"], rows, 2 * WIDTH)
+    gathered = (SPLIT["z"], rows, 2 * WIDTH)
     cached = (SPLIT["z"], SPLIT["x"], rows, WIDTH)
     shape = jax.ShapeDtypeStruct(cached, BF16)
+    first = 2 + len(TURNS)
     outs = pl.pallas_call(
         evict_kernel,
-        in_specs=[smem, smem, hbm, hbm, hbm],
+        in_specs=[smem, smem] + [hbm] * (len(TURNS) + 2),
         out_specs=[hbm, hbm],
         out_shape=[shape, shape],
-        input_output_aliases={3: 0, 4: 1},
+        input_output_aliases={first: 0, first + 1: 1},
         scratch_shapes=[
-            pltpu.VMEM(gathered, BF16),
-            pltpu.SemaphoreType.DMA((1 + 2 * SPLIT["x"],)),
+            pltpu.VMEM((len(TURNS),) + gathered, BF16),
+            pltpu.SemaphoreType.DMA((3 * len(TURNS),)),
         ],
         compiler_params=pltpu.CompilerParams(vmem_limit_bytes=60 * 2**20),
         name="evict",
-    )(owner, evictor, kv.reshape(gathered), next_key.reshape(cached), next_value.reshape(cached))
+    )(
+        owner,
+        evictor,
+        *[block.reshape(gathered) for block in blocks],
+        next_key.reshape(cached),
+        next_value.reshape(cached),
+    )
     return [out.reshape(CACHE, WIDTH) for out in outs]
+
+
+def pick_kernel(sheet_ref, after_ref, kv_ref):
+    kv_ref[...] = sheet_ref[:, WIDTH:]
+
+
+def pick(sheet, after):
+    vmem = pl.BlockSpec(memory_space=pltpu.VMEM)
+    return pl.pallas_call(
+        pick_kernel,
+        in_specs=[vmem, pl.BlockSpec(memory_space=pl.ANY)],
+        out_specs=vmem,
+        out_shape=jax.ShapeDtypeStruct((sheet.shape[0], 2 * WIDTH), BF16),
+        name="pick",
+    )(sheet, after)
 
 
 def spread(block, axis):
@@ -245,11 +275,13 @@
     owner = lax.axis_index(CTX).astype(I32).reshape(1)
     fresh = jnp.concatenate([fresh_query, fresh_key, fresh_value], axis=1)
     sheet = spread(fresh, SHEET).reshape(-1, 3 * WIDTH)
-    kv = lax.all_gather(sheet[:, WIDTH:], "x", axis=0, tiled=True)
     queries = spread(sheet[:, :WIDTH], "x").reshape(TOKENS, WIDTH)
     msg, next_key, next_value = attend(
         owner, age_slope, queries, cache_key, cache_value, fresh_key, fresh_value, slot_owner.reshape(1, OWNERS)
     )
+    kv = [pick(sheet, msg)]
+    for turn in TURNS[1:]:
+        kv.append(lax.ppermute(kv[0], "x", [(i, i ^ turn) for i in range(SPLIT["x"])]))
     msg = lax.all_to_all(msg, ("x",) + SHEET, 0, 0, tiled=True)
     gated, squares = merge(timestep, msg, time_gate)
     squares = lax.all_to_all(squares, HEAD, 0, 0, tiled=True)

time: 125 us -> 112 us (0.90)
  between operations: 15.4 us -> 2.07 us
  waiting for transfers between devices: 36 us -> 25 us
  starting transfers between devices: 25.7 us -> 34.6 us
  Pallas kernels: 9.63 us -> 11.5 us
    all_to_all x1, waiting for transfers between devices: 23.3 us -> 12.5 us  [body(): msg = lax.all_to_all(msg, ('x',) + SHEET, 0, 0, tiled=True)]
    ppermute x0 -> x3, starting transfers between devices: none -> 9.13 us  [body(): lax.ppermute(kv[0], 'x', [(i, i ^ turn) for i in range(SPLIT['x'])])]
    pallas_call x1 -> x2, Pallas kernels: 0.13 us -> 1.98 us  [the longest x1 1.87 us: pick(): pl.pallas_call(pick_kernel, in_specs=[vmem, pl.BlockSpec(memory_space=pl....]
    unnamed x14 -> x22, local copies, waits for them, and re-layouts: 0.03 us -> 1.64 us
  transfers between devices with their start and end apart: 4 -> 6, of which waited for: 3 -> 3; matrix products, arithmetic and copies ran while one was open for 1% -> 0% of each run, Pallas kernels for 8% -> 3%
where the time goes in v3:
time: 112 us; the launch traced here: 111 us
  starting transfers between devices  34.6 us (31%)
  blocking collectives  33.9 us (30%)
  waiting for transfers between devices  25 us (22%)
  Pallas kernels  11.5 us (10%)
  local copies, waits for them, and re-layouts  2.8 us (2%)
  between operations  2.07 us (2%)
  other arithmetic  1.46 us (1%)
    all_to_all x1, blocking collectives, spread(): return lax.all_to_all(sent, axis, 0, 0, tiled=True)  33.9 us
    all_to_all x1, waiting for transfers between devices, body(): msg = lax.all_to_all(msg, ('x',) + SHEET, 0, 0, tiled=True)  12.5 us
    all_to_all x1, starting transfers between devices, body(): msg = lax.all_to_all(msg, ('x',) + SHEET, 0, 0, tiled=True)  11.1 us
    all_to_all x1, starting transfers between devices, body(): squares = lax.all_to_all(squares, HEAD, 0, 0, tiled=True)  10.2 us
    all_to_all x1, waiting for transfers between devices, spread(): return lax.all_to_all(sent, axis, 0, 0, tiled=True)  9.52 us
    ppermute x3, starting transfers between devices, body(): lax.ppermute(kv[0], 'x', [(i, i ^ turn) for i in range(SPLIT['x'])])  9.13 us
    pallas_call x1, Pallas kernels, attend(): pl.pallas_call(attend_kernel, grid=(TOKENS // BLOCK,), in_specs=[smem, sm...  8.06 us
    all_to_all x1, starting transfers between devices, spread(): return lax.all_to_all(sent, axis, 0, 0, tiled=True)  4.16 us
  transfers between devices with their start and end apart: 6, of which 3 were waited for; matrix products, arithmetic and copies ran while one was open for 0% of the time, Pallas kernels for 3%

profile of v3, /device:TPU:1, one launch (start us, length us, event | category | flops | bytes accessed | tf_op | source)
XLA Modules:
  0.0 111.4 jit_solution(14395968176402793318)
XLA Ops:
  0.6 0.7 pad_maximum_fusion
  1.4 33.9 %all_to_all.20 = bf16[16,16,1152]{2,1,0:T(8,128)(2,1)S(1)} all-to-all(bf16[16,16,1152]{2,1,0:T(8,128)(2,1)S(1)} %broadcast_in_dim.4), channel_id=1, replica_groups=mesh['z'=8,'x'=4,'yh'=2,'yl'=4,'core'=2] {'z','yh'}, dimensions={0} | all-to-all | bytes 1179648 | tf_op jit(solution)/shard_map/all_to_all | solution.py:260
  35.4 0.0 copy-start.7
  35.4 1.1 broadcast_in_dim.5
  36.5 0.0 copy-done.7
  36.5 0.0 copy-start.3
  36.5 0.0 copy-start.4
  36.5 0.0 copy-start.6
  36.5 4.2 %all-to-all-start.1 = ((bf16[4,256,384]{2,1,0:T(8,128)(2,1)}), bf16[4,256,384]{2,1,0:T(8,128)(2,1)S(1)}, u32[]{:S(2)}, u32[]{:S(2)}) async-start(bf16[4,256,384]{2,1,0:T(8,128)(2,1)} %broadcast_in_dim.5), calls=%async_computation.1 | async-start | bytes 1572864 | tf_op jit(solution)/shard_map/all_to_all | solution.py:260
  40.6 0.0 copy-start.1
  40.6 0.0 copy-start.2
  40.7 9.5 %all-to-all-done.1 = bf16[4,256,384]{2,1,0:T(8,128)(2,1)S(1)} async-done(((bf16[4,256,384]{2,1,0:T(8,128)(2,1)}), bf16[4,256,384]{2,1,0:T(8,128)(2,1)S(1)}, u32[]{:S(2)}, u32[]{:S(2)}) %all-to-all-start.1) | async-done | bytes 786464 | tf_op jit(solution)/shard_map/all_to_all | solution.py:260
  50.2 0.0 copy-start.5
  50.2 0.0 copy-done.3
  50.2 0.0 copy-done.4
  50.2 0.0 copy-done.6
  50.2 0.0 copy-done.1
  50.2 0.0 copy-done.2
  50.2 0.6 copy-done.5
  50.8 8.1 %attend.1 = (s16[64,56,128]{2,1,0:T(8,128)(2,1)}, bf16[1024,384]{1,0:T(8,128)(2,1)}, bf16[1024,384]{1,0:T(8,128)(2,1)}) custom-call(s32[1]{0:T(128)} %bitcast.owner_ref, f32[3]{0:T(128)S(1)} %copy-done.5, bf16[1024,384]{1,0:T(8,128)(2,1)S(1)} %bitcast.12, bf16[1024,384]{1,0:T(8,128)(2,1)S(1)} %copy-done.3, bf16[1024,384]{1,0:T(8,128)(2,1)S(1)} %copy-done.4, ...), custom_call_target="tpu_custom_call" | custom-call | flops 2453667840 | bytes 1572864 | tf_op jit(solution)/shard_map/attend/pallas_call | solution.py:112
  58.9 11.1 %all-to-all-start.2 = ((s16[64,56,128]{2,1,0:T(8,128)(2,1)}), s16[64,56,128]{2,1,0:T(8,128)(2,1)S(1)}, u32[]{:S(2)}, u32[]{:S(2)}) async-start(s16[64,56,128]{2,1,0:T(8,128)(2,1)} %get-tuple-element.10.after_ref), calls=%async_computation.2 | async-start | bytes 1835008 | tf_op jit(solution)/shard_map/all_to_all | solution.py:285
  70.0 0.0 copy-start
  70.0 1.9 %pick.1 = bf16[256,768]{1,0:T(8,128)(2,1)} custom-call(bf16[256,1152]{1,0:T(8,128)(2,1)} %bitcast.15, s16[64,56,128]{2,1,0:T(8,128)(2,1)} %get-tuple-element.10.after_ref), custom_call_target="tpu_custom_call" | custom-call | tf_op jit(solution)/shard_map/pick/pallas_call | solution.py:248
  71.9 4.5 %collective-permute-start.2 = (bf16[256,768]{1,0:T(8,128)(2,1)}, bf16[256,768]{1,0:T(8,128)(2,1)S(1)}, u32[]{:S(2)}, u32[]{:S(2)}) collective-permute-start(bf16[256,768]{1,0:T(8,128)(2,1)} %pick.1), channel_id=1, source_target_pairs={{0,32},{16,48},{32,0},{48,16},{1,33},{17,49},{33,1},{49,17},{2,34}... | collective-permute-start | bytes 1179656 | tf_op jit(solution)/shard_map/ppermute | solution.py:284
  76.4 2.7 %collective-permute-start.1 = (bf16[256,768]{1,0:T(8,128)(2,1)}, bf16[256,768]{1,0:T(8,128)(2,1)S(1)}, u32[]{:S(2)}, u32[]{:S(2)}) collective-permute-start(bf16[256,768]{1,0:T(8,128)(2,1)} %pick.1), channel_id=1, source_target_pairs={{0,48},{16,32},{32,16},{48,0},{1,49},{17,33},{33,17},{49,1},{2,50}... | collective-permute-start | bytes 1179656 | tf_op jit(solution)/shard_map/ppermute | solution.py:284
  79.1 1.9 %collective-permute-start = (bf16[256,768]{1,0:T(8,128)(2,1)}, bf16[256,768]{1,0:T(8,128)(2,1)S(1)}, u32[]{:S(2)}, u32[]{:S(2)}) collective-permute-start(bf16[256,768]{1,0:T(8,128)(2,1)} %pick.1), channel_id=1, source_target_pairs={{0,16},{16,0},{32,48},{48,32},{1,17},{17,1},{33,49},{49,33},{2,18}... | collective-permute-start | bytes 1179656 | tf_op jit(solution)/shard_map/ppermute | solution.py:284
  81.7 12.5 %all-to-all-done.2.msg_ref = s16[64,56,128]{2,1,0:T(8,128)(2,1)S(1)} async-done(((s16[64,56,128]{2,1,0:T(8,128)(2,1)}), s16[64,56,128]{2,1,0:T(8,128)(2,1)S(1)}, u32[]{:S(2)}, u32[]{:S(2)}) %all-to-all-start.2) | async-done | bytes 917536 | tf_op jit(solution)/shard_map/all_to_all | solution.py:285
  94.2 0.0 copy-done
  94.2 1.5 %merge.1 = (f32[16,384]{1,0:T(8,128)S(1)}, f32[8,1,128]{2,1,0:T(1,128)}) custom-call(s32[1]{0:T(128)S(6)} %copy.18.time_ref, s16[64,56,128]{2,1,0:T(8,128)(2,1)S(1)} %all-to-all-done.2.msg_ref, f32[50,384]{1,0:T(8,128)S(1)} %copy-done), custom_call_target="tpu_custom_call" | custom-call | tf_op jit(solution)/shard_map/merge/pallas_call | solution.py:170
  95.7 10.2 %all-to-all-start.3 = ((f32[8,1,128]{2,1,0:T(1,128)}), f32[8,1,128]{2,1,0:T(1,128)S(1)}, u32[]{:S(2)}, u32[]{:S(2)}) async-start(f32[8,1,128]{2,1,0:T(1,128)} %get-tuple-element.12), calls=%async_computation.3 | async-start | bytes 8192 | tf_op jit(solution)/shard_map/all_to_all | solution.py:287
  106.6 0.0 collective-permute-done.2
  106.6 0.0 copy-start.8
  106.6 0.0 collective-permute-done.1
  106.6 0.0 copy-start.9
  106.6 0.0 collective-permute-done
  106.6 0.0 copy-start.10
  106.7 0.7 copy-done.8
  107.4 0.1 copy-done.9
  107.5 0.1 copy-done.10
  107.6 0.1 evict.1
  107.8 3.0 %all-to-all-done.3 = f32[8,1,128]{2,1,0:T(1,128)S(1)} async-done(((f32[8,1,128]{2,1,0:T(1,128)}), f32[8,1,128]{2,1,0:T(1,128)S(1)}, u32[]{:S(2)}, u32[]{:S(2)}) %all-to-all-start.3) | async-done | bytes 4128 | tf_op jit(solution)/shard_map/all_to_all | solution.py:287
  110.8 0.7 multiply_convert_fusion
  (4 shorter events, 0.1 us)
Async XLA Ops:
  35.4 1.1 %copy-start.7 = (bf16[16,16,1152]{2,1,0:T(8,128)(2,1)}, bf16[16,16,1152]{2,1,0:T(8,128)(2,1)S(1)}, u32[]{:S(2)}) copy-start(bf16[16,16,1152]{2,1,0:T(8,128)(2,1)S(1)} %all_to_all.20) | copy-start | bytes 1769476
  36.5 13.7 %copy-start.3 = (bf16[1024,384]{1,0:T(8,128)(2,1)S(1)}, bf16[1024,384]{1,0:T(8,128)(2,1)}, u32[]{:S(2)}) copy-start(bf16[1024,384]{1,0:T(8,128)(2,1)} %k_ref.1) | copy-start | bytes 2359300
  36.5 13.7 %copy-start.4 = (bf16[1024,384]{1,0:T(8,128)(2,1)S(1)}, bf16[1024,384]{1,0:T(8,128)(2,1)}, u32[]{:S(2)}) copy-start(bf16[1024,384]{1,0:T(8,128)(2,1)} %v_ref.1) | copy-start | bytes 2359300
  36.5 13.7 %copy-start.6 = (s32[64]{0:T(128)S(1)}, s32[64]{0:T(128)}, u32[]{:S(2)}) copy-start(s32[64]{0:T(128)} %param.15) | copy-start | bytes 772
  36.5 13.7 %all-to-all-start.1 = ((bf16[4,256,384]{2,1,0:T(8,128)(2,1)}), bf16[4,256,384]{2,1,0:T(8,128)(2,1)S(1)}, u32[]{:S(2)}, u32[]{:S(2)}) async-start(bf16[4,256,384]{2,1,0:T(8,128)(2,1)} %broadcast_in_dim.5), calls=%async_computation.1 | async-start | bytes 1572864 | tf_op jit(solution)/shard_map/all_to_all | solution.py:260
  40.6 9.5 %copy-start.1 = (bf16[16,384]{1,0:T(8,128)(2,1)S(1)}, bf16[16,384]{1,0:T(8,128)(2,1)}, u32[]{:S(2)}) copy-start(bf16[16,384]{1,0:T(8,128)(2,1)} %fv_ref.1) | copy-start | bytes 36868
  40.6 9.6 %copy-start.2 = (bf16[16,384]{1,0:T(8,128)(2,1)S(1)}, bf16[16,384]{1,0:T(8,128)(2,1)}, u32[]{:S(2)}) copy-start(bf16[16,384]{1,0:T(8,128)(2,1)} %fk_ref.1) | copy-start | bytes 36868
  50.2 0.7 copy-start.5
  58.9 35.3 %all-to-all-start.2 = ((s16[64,56,128]{2,1,0:T(8,128)(2,1)}), s16[64,56,128]{2,1,0:T(8,128)(2,1)S(1)}, u32[]{:S(2)}, u32[]{:S(2)}) async-start(s16[64,56,128]{2,1,0:T(8,128)(2,1)} %get-tuple-element.10.after_ref), calls=%async_computation.2 | async-start | bytes 1835008 | tf_op jit(solution)/shard_map/all_to_all | solution.py:285
  70.0 24.2 %copy-start = (f32[50,384]{1,0:T(8,128)S(1)}, f32[50,384]{1,0:T(8,128)}, u32[]{:S(2)}) copy-start(f32[50,384]{1,0:T(8,128)} %gate_ref.1) | copy-start | bytes 230404
  71.9 34.7 %collective-permute-start.2 = (bf16[256,768]{1,0:T(8,128)(2,1)}, bf16[256,768]{1,0:T(8,128)(2,1)S(1)}, u32[]{:S(2)}, u32[]{:S(2)}) collective-permute-start(bf16[256,768]{1,0:T(8,128)(2,1)} %pick.1), channel_id=1, source_target_pairs={{0,32},{16,48},{32,0},{48,16},{1,33},{17,49},{33,1},{49,17},{2,34}... | collective-permute-start | bytes 1179656 | tf_op jit(solution)/shard_map/ppermute | solution.py:284
  76.4 30.2 %collective-permute-start.1 = (bf16[256,768]{1,0:T(8,128)(2,1)}, bf16[256,768]{1,0:T(8,128)(2,1)S(1)}, u32[]{:S(2)}, u32[]{:S(2)}) collective-permute-start(bf16[256,768]{1,0:T(8,128)(2,1)} %pick.1), channel_id=1, source_target_pairs={{0,48},{16,32},{32,16},{48,0},{1,49},{17,33},{33,17},{49,1},{2,50}... | collective-permute-start | bytes 1179656 | tf_op jit(solution)/shard_map/ppermute | solution.py:284
  79.1 27.5 %collective-permute-start = (bf16[256,768]{1,0:T(8,128)(2,1)}, bf16[256,768]{1,0:T(8,128)(2,1)S(1)}, u32[]{:S(2)}, u32[]{:S(2)}) collective-permute-start(bf16[256,768]{1,0:T(8,128)(2,1)} %pick.1), channel_id=1, source_target_pairs={{0,16},{16,0},{32,48},{48,32},{1,17},{17,1},{33,49},{49,33},{2,18}... | collective-permute-start | bytes 1179656 | tf_op jit(solution)/shard_map/ppermute | solution.py:284
  95.7 15.0 %all-to-all-start.3 = ((f32[8,1,128]{2,1,0:T(1,128)}), f32[8,1,128]{2,1,0:T(1,128)S(1)}, u32[]{:S(2)}, u32[]{:S(2)}) async-start(f32[8,1,128]{2,1,0:T(1,128)} %get-tuple-element.12), calls=%async_computation.3 | async-start | bytes 8192 | tf_op jit(solution)/shard_map/all_to_all | solution.py:287
  106.6 0.8 copy-start.8
  106.6 0.9 copy-start.9
  106.6 1.0 copy-start.10

commit v4 on v3

--- a/solution.py
+++ b/solution.py
@@ -1,3 +1,4 @@
+import functools
 import math
 
 import jax
@@ -18,8 +19,7 @@
 WIDTH = HEADS * DIM
 TOKENS = OWNERS * ROWS
 CACHE = 1024
-BLOCK = 1024
-SENDERS = BLOCK // ROWS
+SENDERS = OWNERS // 4
 TURNS = (0, 1, 3, 2)
 MSG_ROWS = HEADS * ROWS + 8
 FEATURES = 3072
@@ -55,83 +55,95 @@
     return both[:, :DIM] / total, largest + jnp.log2(total)
 
 
-def attend_kernel(owner_ref, slope_ref, q_ref, k_ref, v_ref, fk_ref, fv_ref, slots_ref, msg_ref, nk_ref, nv_ref, sem):
-    step = pl.program_id(0)
-    copies = [
-        pltpu.make_async_copy(k_ref, nk_ref, sem.at[0]),
-        pltpu.make_async_copy(v_ref, nv_ref, sem.at[1]),
-    ]
-
-    @pl.when(step == 0)
-    def _():
-        for copy in copies:
-            copy.start()
-
+def attend_kernel(turns, owner_ref, slope_ref, k_ref, v_ref, fk_ref, fv_ref, slots_ref, *refs):
+    q_refs, (held, sem) = refs[: len(turns)], refs[-2:]
+    if turns[0] == 0:
+        msg_ref, nk_ref, nv_ref = refs[len(turns) : -2]
+        copies = [
+            pltpu.make_async_copy(k_ref, nk_ref, sem.at[0]),
+            pltpu.make_async_copy(v_ref, nv_ref, sem.at[1]),
+        ]
+    else:
+        msg_ref, copies = refs[-3], []
+    for copy in copies:
+        copy.start()
+    tokens = len(turns) * SENDERS * ROWS
+    senders = len(turns) * SENDERS
     slots = slots_ref[...]
     slot_ids = lax.broadcasted_iota(I32, slots.shape, 1)
     rank = jnp.sum(jnp.where(slots == owner_ref[0], slot_ids, 0).astype(F32), axis=1, keepdims=True)
     age = (rank + 1.0) / OWNERS
-    piece = lax.broadcasted_iota(I32, (BLOCK, DIM), 1) % 64
-    stats = jnp.zeros((BLOCK, DIM), I32)
+    piece = lax.broadcasted_iota(I32, (tokens, DIM), 1) % 64
+    stats = jnp.zeros((tokens, DIM), I32)
     for h in range(HEADS):
         cols = slice(h * DIM, (h + 1) * DIM)
         part, weight = softmax_part(
-            q_ref[:, cols],
+            jnp.concatenate([q_ref[:, cols] for q_ref in q_refs], axis=0),
             k_ref[:, cols],
             v_ref[:, cols],
             fk_ref[:, cols],
             fv_ref[:, cols],
-            age * (slope_ref[h] * LOG2E),
+            age * (slope_ref[:, h : h + 1] * LOG2E),
         )
         reach = jnp.max(jnp.abs(part), axis=1, keepdims=True)
         power = jnp.floor(jnp.log2(jnp.maximum(reach, 1e-30))) + 1.0
         codes = jnp.round(part * (jnp.exp2(-power) * TOP)).astype(I32)
-        msg_ref[:, h * ROWS : (h + 1) * ROWS, :] = codes.astype(I16).reshape(SENDERS, ROWS, DIM)
+        held[:, h * ROWS : (h + 1) * ROWS, :] = codes.astype(I16).reshape(senders, ROWS, DIM)
         fixed = jnp.round(weight * 65536.0).astype(I32)
         high = (fixed + 32768) >> 16
         low = fixed - (high << 16)
         stats = jnp.where(piece == h, high, stats)
         stats = jnp.where(piece == 8 + h, low, stats)
         stats = jnp.where(piece == 16 + h, power.astype(I32), stats)
-    halves = stats.reshape(SENDERS, 2, 8, DIM)
-    early = lax.broadcasted_iota(I32, (SENDERS, 8, DIM), 2) < 64
+    halves = stats.reshape(senders, 2, 8, DIM)
+    early = lax.broadcasted_iota(I32, (senders, 8, DIM), 2) < 64
     packed = jnp.where(early, halves[:, 0], halves[:, 1])
-    msg_ref[:, HEADS * ROWS :, :] = packed.astype(I16)
-
-    @pl.when(step == pl.num_programs(0) - 1)
-    def _():
-        for copy in copies:
-            copy.wait()
-
-
-def attend(owner, slope, query, key, value, fresh_key, fresh_value, slots):
-    smem = pl.BlockSpec(memory_space=pltpu.SMEM)
+    held[:, HEADS * ROWS :, :] = packed.astype(I16)
+    for at, turn in enumerate(turns):
+        x = ((owner_ref[0] >> 1) & 3) ^ turn
+        copies.append(
+            pltpu.make_async_copy(
+                held.at[at * SENDERS : (at + 1) * SENDERS],
+                msg_ref.at[pl.ds(x * SENDERS, SENDERS)],
+                sem.at[2 + at],
+            )
+        )
+        copies[-1].start()
+
+    for copy in copies:
+        copy.wait()
+
+
+def attend(turns, owner, slope, queries, key, value, fresh_key, fresh_value, slots, msg=None):
+    vmem = pl.BlockSpec(memory_space=pltpu.VMEM)
     hbm = pl.BlockSpec(memory_space=pl.ANY)
-    whole = lambda shape: pl.BlockSpec(shape, lambda i: (0,) * len(shape))
-    pairs = TOKENS * (CACHE + ROWS) * HEADS
+    pairs = len(turns) * SENDERS * ROWS * (CACHE + ROWS) * HEADS
+    args = [owner, slope, key, value, fresh_key, fresh_value, slots, *queries]
+    in_specs = [pl.BlockSpec(memory_space=pltpu.SMEM)] + [vmem] * (6 + len(turns))
+    out_shape = [jax.ShapeDtypeStruct((OWNERS, MSG_ROWS, DIM), I16)]
+    aliases = {}
+    if msg is None:
+        out_shape += [jax.ShapeDtypeStruct((CACHE, WIDTH), BF16)] * 2
+    else:
+        aliases = {len(args): 0}
+        args.append(msg)
+        in_specs.append(hbm)
     return pl.pallas_call(
-        attend_kernel,
-        grid=(TOKENS // BLOCK,),
-        in_specs=[
-            smem,
-            smem,
-            pl.BlockSpec((BLOCK, WIDTH), lambda i: (i, 0)),
-            whole((CACHE, WIDTH)),
-            whole((CACHE, WIDTH)),
-            whole((ROWS, WIDTH)),
-            whole((ROWS, WIDTH)),
-            whole((1, OWNERS)),
+        functools.partial(attend_kernel, turns),
+        in_specs=in_specs,
+        out_specs=[hbm] * len(out_shape),
+        out_shape=out_shape,
+        input_output_aliases=aliases,
+        scratch_shapes=[
+            pltpu.VMEM((len(turns) * SENDERS, MSG_ROWS, DIM), I16),
+            pltpu.SemaphoreType.DMA((2 + len(turns),)),
         ],
-        out_specs=[pl.BlockSpec((SENDERS, MSG_ROWS, DIM), lambda i: (i, 0, 0)), hbm, hbm],
-        out_shape=[jax.ShapeDtypeStruct((OWNERS, MSG_ROWS, DIM), I16)]
-        + [jax.ShapeDtypeStruct((CACHE, WIDTH), BF16)] * 2,
-        scratch_shapes=[pltpu.SemaphoreType.DMA((2,))],
         cost_estimate=pl.CostEstimate(
             flops=6 * DIM * pairs, bytes_accessed=4 * CACHE * WIDTH, transcendentals=pairs
         ),
         compiler_params=pltpu.CompilerParams(vmem_limit_bytes=40 * 2**20),
         name="attend",
-    )(owner, slope, query, key, value, fresh_key, fresh_value, slots)
+    )(*args)
 
 
 def merge_kernel(time_ref, msg_ref, gate_ref, gated_ref, square_ref):
@@ -260,6 +272,11 @@
     return lax.all_to_all(sent, axis, 0, 0, tiled=True)
 
 
+def around(block):
+    ways = [[(i, i ^ turn) for i in range(SPLIT["x"])] for turn in TURNS[1:]]
+    return [block] + [lax.ppermute(block, "x", way) for way in ways]
+
+
 def body(
     fresh_query,
     fresh_key,
@@ -275,13 +292,12 @@
     owner = lax.axis_index(CTX).astype(I32).reshape(1)
     fresh = jnp.concatenate([fresh_query, fresh_key, fresh_value], axis=1)
     sheet = spread(fresh, SHEET).reshape(-1, 3 * WIDTH)
-    queries = spread(sheet[:, :WIDTH], "x").reshape(TOKENS, WIDTH)
-    msg, next_key, next_value = attend(
-        owner, age_slope, queries, cache_key, cache_value, fresh_key, fresh_value, slot_owner.reshape(1, OWNERS)
-    )
-    kv = [pick(sheet, msg)]
-    for turn in TURNS[1:]:
-        kv.append(lax.ppermute(kv[0], "x", [(i, i ^ turn) for i in range(SPLIT["x"])]))
+    queries = around(sheet[:, :WIDTH])
+    slope = age_slope.reshape(1, HEADS)
+    cache = (cache_key, cache_value, fresh_key, fresh_value, slot_owner.reshape(1, OWNERS))
+    msg, next_key, next_value = attend(TURNS[:1], owner, slope, queries[:1], *cache)
+    (msg,) = attend(TURNS[1:], owner, slope, queries[1:], *cache, msg)
+    kv = around(pick(sheet, msg))
     msg = lax.all_to_all(msg, ("x",) + SHEET, 0, 0, tiled=True)
     gated, squares = merge(timestep, msg, time_gate)
     squares = lax.all_to_all(squares, HEAD, 0, 0, tiled=True)

time: 112 us -> 110 us (0.982)
  waiting for transfers between devices: 25 us -> 14.6 us
  starting transfers between devices: 34.6 us -> 41.8 us
  Pallas kernels: 11.5 us -> 13.1 us
    all_to_all x1 -> x0, waiting for transfers between devices: 9.52 us -> none  [spread(): return lax.all_to_all(sent, axis, 0, 0, tiled=True)]
    ppermute x3 -> x6, starting transfers between devices: 9.13 us -> 18.5 us  [around(): return [block] + [lax.ppermute(block, 'x', way) for way in ways]]
    all_to_all x1 -> x0, starting transfers between devices: 4.16 us -> none  [spread(): return lax.all_to_all(sent, axis, 0, 0, tiled=True)]
    all_to_all x1, starting transfers between devices: 10.2 us -> 12 us  [body(): squares = lax.all_to_all(squares, HEAD, 0, 0, tiled=True)]
    all_to_all x1, waiting for transfers between devices: 12.5 us -> 10.7 us  [body(): msg = lax.all_to_all(msg, ('x',) + SHEET, 0, 0, tiled=True)]
    pallas_call x1 -> x2, Pallas kernels: 8.06 us -> 9.66 us  [attend(): pl.pallas_call(functools.partial(attend_kernel, turns), in_specs=in_specs...]
  transfers between devices with their start and end apart: 6 -> 8, of which waited for: 3 -> 3; matrix products, arithmetic and copies ran while one was open for 0% -> 0% of each run, Pallas kernels for 3% -> 6%
where the time goes in v4:
time: 110 us; the launch traced here: 109 us
  starting transfers between devices  41.8 us (38%)
  blocking collectives  34.1 us (31%)
  waiting for transfers between devices  14.6 us (13%)
  Pallas kernels  13.1 us (12%)
  between operations  2.17 us (2%)
  local copies, waits for them, and re-layouts  1.75 us (2%)
  other arithmetic  1.46 us (1%)
    all_to_all x1, blocking collectives, spread(): return lax.all_to_all(sent, axis, 0, 0, tiled=True)  34.1 us
    ppermute x6, starting transfers between devices, around(): return [block] + [lax.ppermute(block, 'x', way) for way in ways]  18.5 us
    all_to_all x1, starting transfers between devices, body(): squares = lax.all_to_all(squares, HEAD, 0, 0, tiled=True)  12 us
    all_to_all x1, starting transfers between devices, body(): msg = lax.all_to_all(msg, ('x',) + SHEET, 0, 0, tiled=True)  11.3 us
    all_to_all x1, waiting for transfers between devices, body(): msg = lax.all_to_all(msg, ('x',) + SHEET, 0, 0, tiled=True)  10.7 us
    pallas_call x2, Pallas kernels, attend(): pl.pallas_call(functools.partial(attend_kernel, turns), in_specs=in_specs...  9.66 us
    all_to_all x1, waiting for transfers between devices, body(): squares = lax.all_to_all(squares, HEAD, 0, 0, tiled=True)  2.98 us
  transfers between devices with their start and end apart: 8, of which 3 were waited for; matrix products, arithmetic and copies ran while one was open for 0% of the time, Pallas kernels for 6%

profile of v4, /device:TPU:1, one launch (start us, length us, event | category | flops | bytes accessed | tf_op | source)
XLA Modules:
  0.0 109.1 jit_solution(3138638569549355861)
XLA Ops:
  0.6 0.7 pad_maximum_fusion
  1.4 0.0 copy-start.3
  1.4 0.0 copy-start.4
  1.4 34.1 %all_to_all.15 = bf16[16,16,1152]{2,1,0:T(8,128)(2,1)S(1)} all-to-all(bf16[16,16,1152]{2,1,0:T(8,128)(2,1)S(1)} %broadcast_in_dim.2), channel_id=1, replica_groups=mesh['z'=8,'x'=4,'yh'=2,'yl'=4,'core'=2] {'z','yh'}, dimensions={0} | all-to-all | bytes 1179648 | tf_op jit(solution)/shard_map/all_to_all | solution.py:272
  35.5 0.0 copy-start.7
  35.5 0.0 copy-start.6
  35.5 4.7 %collective-permute-start.2 = (bf16[256,384]{1,0:T(8,128)(2,1)S(1)}, bf16[256,384]{1,0:T(8,128)(2,1)S(1)}, u32[]{:S(2)}, u32[]{:S(2)}) collective-permute-start(bf16[256,384]{1,0:T(8,128)(2,1)S(1)} %slice.8.refs_0_), channel_id=1, source_target_pairs={{0,32},{16,48},{32,0},{48,16},{1,33},{17,49},{33,1},{49,17},{2,34}... | collective-permute-start | bytes 589832 | tf_op jit(solution)/shard_map/ppermute | solution.py:277
  40.2 2.8 %collective-permute-start.1 = (bf16[256,384]{1,0:T(8,128)(2,1)S(1)}, bf16[256,384]{1,0:T(8,128)(2,1)S(1)}, u32[]{:S(2)}, u32[]{:S(2)}) collective-permute-start(bf16[256,384]{1,0:T(8,128)(2,1)S(1)} %slice.8.refs_0_), channel_id=1, source_target_pairs={{0,48},{16,32},{32,16},{48,0},{1,49},{17,33},{33,17},{49,1},{2,50}... | collective-permute-start | bytes 589832 | tf_op jit(solution)/shard_map/ppermute | solution.py:277
  43.0 1.9 %collective-permute-start = (bf16[256,384]{1,0:T(8,128)(2,1)S(1)}, bf16[256,384]{1,0:T(8,128)(2,1)S(1)}, u32[]{:S(2)}, u32[]{:S(2)}) collective-permute-start(bf16[256,384]{1,0:T(8,128)(2,1)S(1)} %slice.8.refs_0_), channel_id=1, source_target_pairs={{0,16},{16,0},{32,48},{48,32},{1,17},{17,1},{33,49},{49,33},{2,18}... | collective-permute-start | bytes 589832 | tf_op jit(solution)/shard_map/ppermute | solution.py:277
  44.9 0.0 copy-start.1
  44.9 0.0 copy-start.2
  44.9 0.0 copy-start.5
  45.0 0.0 copy-done.3
  45.0 0.0 copy-done.4
  45.0 0.0 copy-done.6
  45.0 0.6 copy-done.1
  45.6 0.0 copy-done.2
  45.6 0.0 copy-done.5
  45.6 3.1 %attend.2 = (s16[64,56,128]{2,1,0:T(8,128)(2,1)}, bf16[1024,384]{1,0:T(8,128)(2,1)}, bf16[1024,384]{1,0:T(8,128)(2,1)}) custom-call(s32[1]{0:T(128)} %bitcast.owner_ref, f32[1,3]{1,0:T(1,128)S(1)} %bitcast.12, bf16[1024,384]{1,0:T(8,128)(2,1)S(1)} %copy-done.3, bf16[1024,384]{1,0:T(8,128)(2,1)S(1)} %copy-done.4, bf16[16,384]{1,0:T(8,128)(2,1)S(1)} %copy-done.1, ...), custom_call_target="tpu_custom_call" | custom-call | flops 613416960 | bytes 1572864 | tf_op jit(solution)/shard_map/attend/pallas_call | solution.py:131
  48.7 0.0 copy-done.7
  48.8 0.0 collective-permute-done.2.refs_2_
  48.8 0.0 collective-permute-done.1.refs_1_
  48.8 0.9 collective-permute-done.refs_0_
  49.7 6.6 %attend.3.after_ref = s16[64,56,128]{2,1,0:T(8,128)(2,1)} custom-call(s32[1]{0:T(128)} %bitcast.owner_ref, f32[1,3]{1,0:T(1,128)S(1)} %bitcast.13, bf16[1024,384]{1,0:T(8,128)(2,1)S(1)} %copy-done.3, bf16[1024,384]{1,0:T(8,128)(2,1)S(1)} %copy-done.4, bf16[16,384]{1,0:T(8,128)(2,1)S(1)} %copy-done.1, ...), custom_call_target="tpu_custom_call", output_to_operand_aliasing={{}: (10, {})} | custom-call | flops 1840250880 | bytes 1572864 | tf_op jit(solution)/shard_map/attend/pallas_call | solution.py:131
  56.3 11.3 %all-to-all-start.1 = ((s16[64,56,128]{2,1,0:T(8,128)(2,1)}), s16[64,56,128]{2,1,0:T(8,128)(2,1)S(1)}, u32[]{:S(2)}, u32[]{:S(2)}) async-start(s16[64,56,128]{2,1,0:T(8,128)(2,1)} %attend.3.after_ref), calls=%async_computation.1 | async-start | bytes 1835008 | tf_op jit(solution)/shard_map/all_to_all | solution.py:301
  67.6 0.0 copy-start
  67.6 1.9 %pick.1 = bf16[256,768]{1,0:T(8,128)(2,1)} custom-call(bf16[256,1152]{1,0:T(8,128)(2,1)} %bitcast.17, s16[64,56,128]{2,1,0:T(8,128)(2,1)} %attend.3.after_ref), custom_call_target="tpu_custom_call" | custom-call | tf_op jit(solution)/shard_map/pick/pallas_call | solution.py:260
  69.5 4.5 %collective-permute-start.5 = (bf16[256,768]{1,0:T(8,128)(2,1)}, bf16[256,768]{1,0:T(8,128)(2,1)S(1)}, u32[]{:S(2)}, u32[]{:S(2)}) collective-permute-start(bf16[256,768]{1,0:T(8,128)(2,1)} %pick.1), channel_id=1, source_target_pairs={{0,32},{16,48},{32,0},{48,16},{1,33},{17,49},{33,1},{49,17},{2,34}... | collective-permute-start | bytes 1179656 | tf_op jit(solution)/shard_map/ppermute | solution.py:277
  74.0 2.7 %collective-permute-start.4 = (bf16[256,768]{1,0:T(8,128)(2,1)}, bf16[256,768]{1,0:T(8,128)(2,1)S(1)}, u32[]{:S(2)}, u32[]{:S(2)}) collective-permute-start(bf16[256,768]{1,0:T(8,128)(2,1)} %pick.1), channel_id=1, source_target_pairs={{0,48},{16,32},{32,16},{48,0},{1,49},{17,33},{33,17},{49,1},{2,50}... | collective-permute-start | bytes 1179656 | tf_op jit(solution)/shard_map/ppermute | solution.py:277
  76.7 1.9 %collective-permute-start.3 = (bf16[256,768]{1,0:T(8,128)(2,1)}, bf16[256,768]{1,0:T(8,128)(2,1)S(1)}, u32[]{:S(2)}, u32[]{:S(2)}) collective-permute-start(bf16[256,768]{1,0:T(8,128)(2,1)} %pick.1), channel_id=1, source_target_pairs={{0,16},{16,0},{32,48},{48,32},{1,17},{17,1},{33,49},{49,33},{2,18}... | collective-permute-start | bytes 1179656 | tf_op jit(solution)/shard_map/ppermute | solution.py:277
  79.3 10.7 %all-to-all-done.1.msg_ref = s16[64,56,128]{2,1,0:T(8,128)(2,1)S(1)} async-done(((s16[64,56,128]{2,1,0:T(8,128)(2,1)}), s16[64,56,128]{2,1,0:T(8,128)(2,1)S(1)}, u32[]{:S(2)}, u32[]{:S(2)}) %all-to-all-start.1) | async-done | bytes 917536 | tf_op jit(solution)/shard_map/all_to_all | solution.py:301
  90.0 0.0 copy-done
  90.0 1.5 %merge.1 = (f32[16,384]{1,0:T(8,128)S(1)}, f32[8,1,128]{2,1,0:T(1,128)}) custom-call(s32[1]{0:T(128)S(6)} %copy.20.time_ref, s16[64,56,128]{2,1,0:T(8,128)(2,1)S(1)} %all-to-all-done.1.msg_ref, f32[50,384]{1,0:T(8,128)S(1)} %copy-done), custom_call_target="tpu_custom_call" | custom-call | tf_op jit(solution)/shard_map/merge/pallas_call | solution.py:182
  91.5 12.0 %all-to-all-start.2 = ((f32[8,1,128]{2,1,0:T(1,128)}), f32[8,1,128]{2,1,0:T(1,128)S(1)}, u32[]{:S(2)}, u32[]{:S(2)}) async-start(f32[8,1,128]{2,1,0:T(1,128)} %get-tuple-element.12), calls=%async_computation.2 | async-start | bytes 8192 | tf_op jit(solution)/shard_map/all_to_all | solution.py:303
  104.2 0.0 collective-permute-done.5
  104.2 0.0 copy-start.8
  104.2 0.0 collective-permute-done.4
  104.2 0.0 copy-start.9
  104.2 0.0 collective-permute-done.3
  104.3 0.0 copy-start.10
  104.3 0.7 copy-done.8
  105.0 0.1 copy-done.9
  105.1 0.1 copy-done.10
  105.2 0.1 evict.1
  105.4 3.0 %all-to-all-done.2 = f32[8,1,128]{2,1,0:T(1,128)S(1)} async-done(((f32[8,1,128]{2,1,0:T(1,128)}), f32[8,1,128]{2,1,0:T(1,128)S(1)}, u32[]{:S(2)}, u32[]{:S(2)}) %all-to-all-start.2) | async-done | bytes 4128 | tf_op jit(solution)/shard_map/all_to_all | solution.py:303
  108.4 0.7 multiply_convert_fusion
  (4 shorter events, 0.1 us)
Async XLA Ops:
  1.4 43.5 %copy-start.3 = (bf16[1024,384]{1,0:T(8,128)(2,1)S(1)}, bf16[1024,384]{1,0:T(8,128)(2,1)}, u32[]{:S(2)}) copy-start(bf16[1024,384]{1,0:T(8,128)(2,1)} %k_ref.3) | copy-start | bytes 2359300
  1.4 43.5 %copy-start.4 = (bf16[1024,384]{1,0:T(8,128)(2,1)S(1)}, bf16[1024,384]{1,0:T(8,128)(2,1)}, u32[]{:S(2)}) copy-start(bf16[1024,384]{1,0:T(8,128)(2,1)} %v_ref.3) | copy-start | bytes 2359300
  35.5 13.2 %copy-start.7 = (bf16[16,16,1152]{2,1,0:T(8,128)(2,1)}, bf16[16,16,1152]{2,1,0:T(8,128)(2,1)S(1)}, u32[]{:S(2)}) copy-start(bf16[16,16,1152]{2,1,0:T(8,128)(2,1)S(1)} %all_to_all.15) | copy-start | bytes 1769476
  35.5 9.5 %copy-start.6 = (s32[64]{0:T(128)S(1)}, s32[64]{0:T(128)}, u32[]{:S(2)}) copy-start(s32[64]{0:T(128)} %param.15) | copy-start | bytes 772
  35.5 13.2 %collective-permute-start.2 = (bf16[256,384]{1,0:T(8,128)(2,1)S(1)}, bf16[256,384]{1,0:T(8,128)(2,1)S(1)}, u32[]{:S(2)}, u32[]{:S(2)}) collective-permute-start(bf16[256,384]{1,0:T(8,128)(2,1)S(1)} %slice.8.refs_0_), channel_id=1, source_target_pairs={{0,32},{16,48},{32,0},{48,16},{1,33},{17,49},{33,1},{49,17},{2,34}... | collective-permute-start | bytes 589832 | tf_op jit(solution)/shard_map/ppermute | solution.py:277
  40.2 8.6 %collective-permute-start.1 = (bf16[256,384]{1,0:T(8,128)(2,1)S(1)}, bf16[256,384]{1,0:T(8,128)(2,1)S(1)}, u32[]{:S(2)}, u32[]{:S(2)}) collective-permute-start(bf16[256,384]{1,0:T(8,128)(2,1)S(1)} %slice.8.refs_0_), channel_id=1, source_target_pairs={{0,48},{16,32},{32,16},{48,0},{1,49},{17,33},{33,17},{49,1},{2,50}... | collective-permute-start | bytes 589832 | tf_op jit(solution)/shard_map/ppermute | solution.py:277
  43.0 6.7 %collective-permute-start = (bf16[256,384]{1,0:T(8,128)(2,1)S(1)}, bf16[256,384]{1,0:T(8,128)(2,1)S(1)}, u32[]{:S(2)}, u32[]{:S(2)}) collective-permute-start(bf16[256,384]{1,0:T(8,128)(2,1)S(1)} %slice.8.refs_0_), channel_id=1, source_target_pairs={{0,16},{16,0},{32,48},{48,32},{1,17},{17,1},{33,49},{49,33},{2,18}... | collective-permute-start | bytes 589832 | tf_op jit(solution)/shard_map/ppermute | solution.py:277
  44.9 0.7 copy-start.1
  44.9 0.7 copy-start.2
  44.9 0.7 copy-start.5
  56.3 33.8 %all-to-all-start.1 = ((s16[64,56,128]{2,1,0:T(8,128)(2,1)}), s16[64,56,128]{2,1,0:T(8,128)(2,1)S(1)}, u32[]{:S(2)}, u32[]{:S(2)}) async-start(s16[64,56,128]{2,1,0:T(8,128)(2,1)} %attend.3.after_ref), calls=%async_computation.1 | async-start | bytes 1835008 | tf_op jit(solution)/shard_map/all_to_all | solution.py:301
  67.6 22.4 %copy-start = (f32[50,384]{1,0:T(8,128)S(1)}, f32[50,384]{1,0:T(8,128)}, u32[]{:S(2)}) copy-start(f32[50,384]{1,0:T(8,128)} %gate_ref.1) | copy-start | bytes 230404
  69.5 34.7 %collective-permute-start.5 = (bf16[256,768]{1,0:T(8,128)(2,1)}, bf16[256,768]{1,0:T(8,128)(2,1)S(1)}, u32[]{:S(2)}, u32[]{:S(2)}) collective-permute-start(bf16[256,768]{1,0:T(8,128)(2,1)} %pick.1), channel_id=1, source_target_pairs={{0,32},{16,48},{32,0},{48,16},{1,33},{17,49},{33,1},{49,17},{2,34}... | collective-permute-start | bytes 1179656 | tf_op jit(solution)/shard_map/ppermute | solution.py:277
  74.0 30.2 %collective-permute-start.4 = (bf16[256,768]{1,0:T(8,128)(2,1)}, bf16[256,768]{1,0:T(8,128)(2,1)S(1)}, u32[]{:S(2)}, u32[]{:S(2)}) collective-permute-start(bf16[256,768]{1,0:T(8,128)(2,1)} %pick.1), channel_id=1, source_target_pairs={{0,48},{16,32},{32,16},{48,0},{1,49},{17,33},{33,17},{49,1},{2,50}... | collective-permute-start | bytes 1179656 | tf_op jit(solution)/shard_map/ppermute | solution.py:277
  76.7 27.5 %collective-permute-start.3 = (bf16[256,768]{1,0:T(8,128)(2,1)}, bf16[256,768]{1,0:T(8,128)(2,1)S(1)}, u32[]{:S(2)}, u32[]{:S(2)}) collective-permute-start(bf16[256,768]{1,0:T(8,128)(2,1)} %pick.1), channel_id=1, source_target_pairs={{0,16},{16,0},{32,48},{48,32},{1,17},{17,1},{33,49},{49,33},{2,18}... | collective-permute-start | bytes 1179656 | tf_op jit(solution)/shard_map/ppermute | solution.py:277
  91.5 16.8 %all-to-all-start.2 = ((f32[8,1,128]{2,1,0:T(1,128)}), f32[8,1,128]{2,1,0:T(1,128)S(1)}, u32[]{:S(2)}, u32[]{:S(2)}) async-start(f32[8,1,128]{2,1,0:T(1,128)} %get-tuple-element.12), calls=%async_computation.2 | async-start | bytes 8192 | tf_op jit(solution)/shard_map/all_to_all | solution.py:303
  104.2 0.8 copy-start.8
  104.2 0.9 copy-start.9
  104.3 1.0 copy-start.10

commit v5 on v4

--- a/solution.py
+++ b/solution.py
@@ -55,7 +55,36 @@
     return both[:, :DIM] / total, largest + jnp.log2(total)
 
 
-def attend_kernel(turns, owner_ref, slope_ref, k_ref, v_ref, fk_ref, fv_ref, slots_ref, *refs):
+def cached_part(query, key, value, penalty):
+    scores = dot_nt(query, key)
+    largest = jnp.max(scores, axis=1, keepdims=True)
+    weights = jnp.exp2((scores - largest) * SCALE2).astype(BF16)
+    both = jnp.dot(weights, with_ones(value), preferred_element_type=F32)
+    total = both[:, DIM:]
+    return both[:, :DIM] / total, largest * SCALE2 - penalty + jnp.log2(total)
+
+
+def encode(part, weight, h, stats):
+    piece = lax.broadcasted_iota(I32, stats.shape, 1) % 64
+    reach = jnp.max(jnp.abs(part), axis=1, keepdims=True)
+    power = jnp.floor(jnp.log2(jnp.maximum(reach, 1e-30))) + 1.0
+    codes = jnp.round(part * (jnp.exp2(-power) * TOP)).astype(I32).astype(I16)
+    fixed = jnp.round(weight * 65536.0).astype(I32)
+    high = (fixed + 32768) >> 16
+    low = fixed - (high << 16)
+    stats = jnp.where(piece == h, high, stats)
+    stats = jnp.where(piece == 8 + h, low, stats)
+    stats = jnp.where(piece == 16 + h, power.astype(I32), stats)
+    return codes.reshape(-1, ROWS, DIM), stats
+
+
+def pack(stats):
+    halves = stats.reshape(-1, 2, 8, DIM)
+    early = lax.broadcasted_iota(I32, (halves.shape[0], 8, DIM), 2) < 64
+    return jnp.where(early, halves[:, 0], halves[:, 1]).astype(I16)
+
+
+def attend_kernel(turns, owner_ref, slope_ref, k_ref, v_ref, sheet_ref, slots_ref, *refs):
     q_refs, (held, sem) = refs[: len(turns)], refs[-2:]
     if turns[0] == 0:
         msg_ref, nk_ref, nv_ref = refs[len(turns) : -2]
@@ -67,38 +96,32 @@
         msg_ref, copies = refs[-3], []
     for copy in copies:
         copy.start()
-    tokens = len(turns) * SENDERS * ROWS
-    senders = len(turns) * SENDERS
     slots = slots_ref[...]
     slot_ids = lax.broadcasted_iota(I32, slots.shape, 1)
     rank = jnp.sum(jnp.where(slots == owner_ref[0], slot_ids, 0).astype(F32), axis=1, keepdims=True)
     age = (rank + 1.0) / OWNERS
-    piece = lax.broadcasted_iota(I32, (tokens, DIM), 1) % 64
-    stats = jnp.zeros((tokens, DIM), I32)
+    mine = (owner_ref[0] >> 3) * 2 + (owner_ref[0] & 1)
+    rows = pl.ds(pl.multiple_of(mine * ROWS, ROWS), ROWS)
+    stats = jnp.zeros((len(turns) * SENDERS * ROWS, DIM), I32)
+    few_stats = jnp.zeros((len(turns) * ROWS, DIM), I32)
     for h in range(HEADS):
         cols = slice(h * DIM, (h + 1) * DIM)
-        part, weight = softmax_part(
-            jnp.concatenate([q_ref[:, cols] for q_ref in q_refs], axis=0),
-            k_ref[:, cols],
-            v_ref[:, cols],
-            fk_ref[:, cols],
-            fv_ref[:, cols],
-            age * (slope_ref[:, h : h + 1] * LOG2E),
-        )
-        reach = jnp.max(jnp.abs(part), axis=1, keepdims=True)
-        power = jnp.floor(jnp.log2(jnp.maximum(reach, 1e-30))) + 1.0
-        codes = jnp.round(part * (jnp.exp2(-power) * TOP)).astype(I32)
-        held[:, h * ROWS : (h + 1) * ROWS, :] = codes.astype(I16).reshape(senders, ROWS, DIM)
-        fixed = jnp.round(weight * 65536.0).astype(I32)
-        high = (fixed + 32768) >> 16
-        low = fixed - (high << 16)
-        stats = jnp.where(piece == h, high, stats)
-        stats = jnp.where(piece == 8 + h, low, stats)
-        stats = jnp.where(piece == 16 + h, power.astype(I32), stats)
-    halves = stats.reshape(senders, 2, 8, DIM)
-    early = lax.broadcasted_iota(I32, (senders, 8, DIM), 2) < 64
-    packed = jnp.where(early, halves[:, 0], halves[:, 1])
-    held[:, HEADS * ROWS :, :] = packed.astype(I16)
+        place = slice(h * ROWS, (h + 1) * ROWS)
+        penalty = age * (slope_ref[:, h : h + 1] * LOG2E)
+        query = jnp.concatenate([q_ref[:, cols] for q_ref in q_refs], axis=0)
+        few = jnp.concatenate([q_ref[rows, cols] for q_ref in q_refs], axis=0)
+        part, weight = cached_part(query, k_ref[:, cols], v_ref[:, cols], penalty)
+        held[:, place, :], stats = encode(part, weight, h, stats)
+        new_key = sheet_ref[:, WIDTH + h * DIM : WIDTH + (h + 1) * DIM]
+        new_value = sheet_ref[:, 2 * WIDTH + h * DIM : 2 * WIDTH + (h + 1) * DIM]
+        part, weight = softmax_part(few, k_ref[:, cols], v_ref[:, cols], new_key, new_value, penalty)
+        codes, few_stats = encode(part, weight, h, few_stats)
+        for at in range(len(turns)):
+            held[at * SENDERS + mine, place, :] = codes[at]
+    held[:, HEADS * ROWS :, :] = pack(stats)
+    packed = pack(few_stats)
+    for at in range(len(turns)):
+        held[at * SENDERS + mine, HEADS * ROWS :, :] = packed[at]
     for at, turn in enumerate(turns):
         x = ((owner_ref[0] >> 1) & 3) ^ turn
         copies.append(
@@ -114,12 +137,12 @@
         copy.wait()
 
 
-def attend(turns, owner, slope, queries, key, value, fresh_key, fresh_value, slots, msg=None):
+def attend(turns, owner, slope, queries, key, value, sheet, slots, msg=None):
     vmem = pl.BlockSpec(memory_space=pltpu.VMEM)
     hbm = pl.BlockSpec(memory_space=pl.ANY)
     pairs = len(turns) * SENDERS * ROWS * (CACHE + ROWS) * HEADS
-    args = [owner, slope, key, value, fresh_key, fresh_value, slots, *queries]
-    in_specs = [pl.BlockSpec(memory_space=pltpu.SMEM)] + [vmem] * (6 + len(turns))
+    args = [owner, slope, key, value, sheet, slots, *queries]
+    in_specs = [pl.BlockSpec(memory_space=pltpu.SMEM)] + [vmem] * (5 + len(turns))
     out_shape = [jax.ShapeDtypeStruct((OWNERS, MSG_ROWS, DIM), I16)]
     aliases = {}
     if msg is None:
@@ -294,7 +317,7 @@
     sheet = spread(fresh, SHEET).reshape(-1, 3 * WIDTH)
     queries = around(sheet[:, :WIDTH])
     slope = age_slope.reshape(1, HEADS)
-    cache = (cache_key, cache_value, fresh_key, fresh_value, slot_owner.reshape(1, OWNERS))
+    cache = (cache_key, cache_value, sheet, slot_owner.reshape(1, OWNERS))
     msg, next_key, next_value = attend(TURNS[:1], owner, slope, queries[:1], *cache)
     (msg,) = attend(TURNS[1:], owner, slope, queries[1:], *cache, msg)
     kv = around(pick(sheet, msg))

time: 110 us -> 109 us (level)
  no operation moved by 1% of the time
where the time goes in v5:
time: 109 us; the launch traced here: 108 us
  starting transfers between devices  41.8 us (38%)
  blocking collectives  34.1 us (31%)
  waiting for transfers between devices  14.5 us (13%)
  Pallas kernels  12.5 us (11%)
  between operations  2.15 us (2%)
  local copies, waits for them, and re-layouts  1.72 us (2%)
  other arithmetic  1.46 us (1%)
    all_to_all x1, blocking collectives, spread(): return lax.all_to_all(sent, axis, 0, 0, tiled=True)  34.1 us
    ppermute x6, starting transfers between devices, around(): return [block] + [lax.ppermute(block, 'x', way) for way in ways]  18.5 us
    all_to_all x1, starting transfers between devices, body(): squares = lax.all_to_all(squares, HEAD, 0, 0, tiled=True)  12 us
    all_to_all x1, starting transfers between devices, body(): msg = lax.all_to_all(msg, ('x',) + SHEET, 0, 0, tiled=True)  11.4 us
    all_to_all x1, waiting for transfers between devices, body(): msg = lax.all_to_all(msg, ('x',) + SHEET, 0, 0, tiled=True)  10.7 us
    pallas_call x2, Pallas kernels, attend(): pl.pallas_call(functools.partial(attend_kernel, turns), in_specs=in_specs...  9.05 us
    all_to_all x1, waiting for transfers between devices, body(): squares = lax.all_to_all(squares, HEAD, 0, 0, tiled=True)  2.97 us
  transfers between devices with their start and end apart: 8, of which 3 were waited for; matrix products, arithmetic and copies ran while one was open for 0% of the time, Pallas kernels for 6%

profile of v5, /device:TPU:1, one launch (start us, length us, event | category | flops | bytes accessed | tf_op | source)
XLA Modules:
  0.0 108.3 jit_solution(475722854799105892)
XLA Ops:
  0.6 0.7 pad_maximum_fusion
  1.4 0.0 copy-start.1
  1.4 0.0 copy-start.2
  1.4 34.1 %all_to_all.15 = bf16[16,16,1152]{2,1,0:T(8,128)(2,1)S(1)} all-to-all(bf16[16,16,1152]{2,1,0:T(8,128)(2,1)S(1)} %broadcast_in_dim.2), channel_id=1, replica_groups=mesh['z'=8,'x'=4,'yh'=2,'yl'=4,'core'=2] {'z','yh'}, dimensions={0} | all-to-all | bytes 1179648 | tf_op jit(solution)/shard_map/all_to_all | solution.py:295
  35.5 0.0 copy-start
  35.5 4.7 %collective-permute-start.2 = (bf16[256,384]{1,0:T(8,128)(2,1)S(1)}, bf16[256,384]{1,0:T(8,128)(2,1)S(1)}, u32[]{:S(2)}, u32[]{:S(2)}) collective-permute-start(bf16[256,384]{1,0:T(8,128)(2,1)S(1)} %slice.8.refs_0_), channel_id=1, source_target_pairs={{0,32},{16,48},{32,0},{48,16},{1,33},{17,49},{33,1},{49,17},{2,34}... | collective-permute-start | bytes 589832 | tf_op jit(solution)/shard_map/ppermute | solution.py:300
  40.2 2.8 %collective-permute-start.1 = (bf16[256,384]{1,0:T(8,128)(2,1)S(1)}, bf16[256,384]{1,0:T(8,128)(2,1)S(1)}, u32[]{:S(2)}, u32[]{:S(2)}) collective-permute-start(bf16[256,384]{1,0:T(8,128)(2,1)S(1)} %slice.8.refs_0_), channel_id=1, source_target_pairs={{0,48},{16,32},{32,16},{48,0},{1,49},{17,33},{33,17},{49,1},{2,50}... | collective-permute-start | bytes 589832 | tf_op jit(solution)/shard_map/ppermute | solution.py:300
  43.0 1.9 %collective-permute-start = (bf16[256,384]{1,0:T(8,128)(2,1)S(1)}, bf16[256,384]{1,0:T(8,128)(2,1)S(1)}, u32[]{:S(2)}, u32[]{:S(2)}) collective-permute-start(bf16[256,384]{1,0:T(8,128)(2,1)S(1)} %slice.8.refs_0_), channel_id=1, source_target_pairs={{0,16},{16,0},{32,48},{48,32},{1,17},{17,1},{33,49},{49,33},{2,18}... | collective-permute-start | bytes 589832 | tf_op jit(solution)/shard_map/ppermute | solution.py:300
  44.9 0.0 copy-start.4
  44.9 0.0 copy-start.5
  44.9 0.0 copy-done.1
  45.0 0.0 copy-done.2
  45.0 0.6 copy-done.4
  45.6 0.0 copy-done.5
  45.6 3.3 %attend.2 = (s16[64,56,128]{2,1,0:T(8,128)(2,1)}, bf16[1024,384]{1,0:T(8,128)(2,1)}, bf16[1024,384]{1,0:T(8,128)(2,1)}) custom-call(s32[1]{0:T(128)} %bitcast.owner_ref, f32[1,3]{1,0:T(1,128)S(1)} %bitcast.16, bf16[1024,384]{1,0:T(8,128)(2,1)S(1)} %copy-done.1, bf16[1024,384]{1,0:T(8,128)(2,1)S(1)} %copy-done.2, bf16[256,1152]{1,0:T(8,128)(2,1)S(1)} %bitcast.13, ...), custom_call_target="tpu_custom_call" | custom-call | flops 613416960 | bytes 1572864 | tf_op jit(solution)/shard_map/attend/pallas_call | solution.py:154
  48.9 0.0 collective-permute-done.2.refs_2_
  48.9 0.0 collective-permute-done.1.refs_1_
  48.9 0.8 collective-permute-done.refs_0_
  49.7 0.0 copy-done
  49.7 5.7 %attend.3.after_ref = s16[64,56,128]{2,1,0:T(8,128)(2,1)} custom-call(s32[1]{0:T(128)} %bitcast.owner_ref, f32[1,3]{1,0:T(1,128)S(1)} %bitcast.17, bf16[1024,384]{1,0:T(8,128)(2,1)S(1)} %copy-done.1, bf16[1024,384]{1,0:T(8,128)(2,1)S(1)} %copy-done.2, bf16[256,1152]{1,0:T(8,128)(2,1)S(1)} %bitcast.14, ...), custom_call_target="tpu_custom_call", output_to_operand_aliasing={{}: (9, {})} | custom-call | flops 1840250880 | bytes 1572864 | tf_op jit(solution)/shard_map/attend/pallas_call | solution.py:154
  55.4 11.4 %all-to-all-start.1 = ((s16[64,56,128]{2,1,0:T(8,128)(2,1)}), s16[64,56,128]{2,1,0:T(8,128)(2,1)S(1)}, u32[]{:S(2)}, u32[]{:S(2)}) async-start(s16[64,56,128]{2,1,0:T(8,128)(2,1)} %attend.3.after_ref), calls=%async_computation.1 | async-start | bytes 1835008 | tf_op jit(solution)/shard_map/all_to_all | solution.py:324
  66.8 0.0 copy-start.3
  66.8 1.9 %pick.1 = bf16[256,768]{1,0:T(8,128)(2,1)} custom-call(bf16[256,1152]{1,0:T(8,128)(2,1)} %bitcast.15, s16[64,56,128]{2,1,0:T(8,128)(2,1)} %attend.3.after_ref), custom_call_target="tpu_custom_call" | custom-call | tf_op jit(solution)/shard_map/pick/pallas_call | solution.py:283
  68.7 4.5 %collective-permute-start.5 = (bf16[256,768]{1,0:T(8,128)(2,1)}, bf16[256,768]{1,0:T(8,128)(2,1)S(1)}, u32[]{:S(2)}, u32[]{:S(2)}) collective-permute-start(bf16[256,768]{1,0:T(8,128)(2,1)} %pick.1), channel_id=1, source_target_pairs={{0,32},{16,48},{32,0},{48,16},{1,33},{17,49},{33,1},{49,17},{2,34}... | collective-permute-start | bytes 1179656 | tf_op jit(solution)/shard_map/ppermute | solution.py:300
  73.2 2.7 %collective-permute-start.4 = (bf16[256,768]{1,0:T(8,128)(2,1)}, bf16[256,768]{1,0:T(8,128)(2,1)S(1)}, u32[]{:S(2)}, u32[]{:S(2)}) collective-permute-start(bf16[256,768]{1,0:T(8,128)(2,1)} %pick.1), channel_id=1, source_target_pairs={{0,48},{16,32},{32,16},{48,0},{1,49},{17,33},{33,17},{49,1},{2,50}... | collective-permute-start | bytes 1179656 | tf_op jit(solution)/shard_map/ppermute | solution.py:300
  75.9 1.9 %collective-permute-start.3 = (bf16[256,768]{1,0:T(8,128)(2,1)}, bf16[256,768]{1,0:T(8,128)(2,1)S(1)}, u32[]{:S(2)}, u32[]{:S(2)}) collective-permute-start(bf16[256,768]{1,0:T(8,128)(2,1)} %pick.1), channel_id=1, source_target_pairs={{0,16},{16,0},{32,48},{48,32},{1,17},{17,1},{33,49},{49,33},{2,18}... | collective-permute-start | bytes 1179656 | tf_op jit(solution)/shard_map/ppermute | solution.py:300
  78.5 10.7 %all-to-all-done.1.msg_ref = s16[64,56,128]{2,1,0:T(8,128)(2,1)S(1)} async-done(((s16[64,56,128]{2,1,0:T(8,128)(2,1)}), s16[64,56,128]{2,1,0:T(8,128)(2,1)S(1)}, u32[]{:S(2)}, u32[]{:S(2)}) %all-to-all-start.1) | async-done | bytes 917536 | tf_op jit(solution)/shard_map/all_to_all | solution.py:324
  89.2 0.0 copy-done.3
  89.3 1.5 %merge.1 = (f32[16,384]{1,0:T(8,128)S(1)}, f32[8,1,128]{2,1,0:T(1,128)}) custom-call(s32[1]{0:T(128)S(6)} %copy.20.time_ref, s16[64,56,128]{2,1,0:T(8,128)(2,1)S(1)} %all-to-all-done.1.msg_ref, f32[50,384]{1,0:T(8,128)S(1)} %copy-done.3), custom_call_target="tpu_custom_call" | custom-call | tf_op jit(solution)/shard_map/merge/pallas_call | solution.py:205
  90.8 12.0 %all-to-all-start.2 = ((f32[8,1,128]{2,1,0:T(1,128)}), f32[8,1,128]{2,1,0:T(1,128)S(1)}, u32[]{:S(2)}, u32[]{:S(2)}) async-start(f32[8,1,128]{2,1,0:T(1,128)} %get-tuple-element.12), calls=%async_computation.2 | async-start | bytes 8192 | tf_op jit(solution)/shard_map/all_to_all | solution.py:326
  103.4 0.0 collective-permute-done.5
  103.4 0.0 copy-start.6
  103.4 0.0 collective-permute-done.4
  103.4 0.0 copy-start.7
  103.4 0.0 collective-permute-done.3
  103.5 0.0 copy-start.8
  103.5 0.7 copy-done.6
  104.2 0.2 copy-done.7
  104.3 0.1 copy-done.8
  104.5 0.1 evict.1
  104.6 3.0 %all-to-all-done.2 = f32[8,1,128]{2,1,0:T(1,128)S(1)} async-done(((f32[8,1,128]{2,1,0:T(1,128)}), f32[8,1,128]{2,1,0:T(1,128)S(1)}, u32[]{:S(2)}, u32[]{:S(2)}) %all-to-all-start.2) | async-done | bytes 4128 | tf_op jit(solution)/shard_map/all_to_all | solution.py:326
  107.6 0.7 multiply_convert_fusion
  (4 shorter events, 0.1 us)
Async XLA Ops:
  1.4 43.5 %copy-start.1 = (bf16[1024,384]{1,0:T(8,128)(2,1)S(1)}, bf16[1024,384]{1,0:T(8,128)(2,1)}, u32[]{:S(2)}) copy-start(bf16[1024,384]{1,0:T(8,128)(2,1)} %k_ref.3) | copy-start | bytes 2359300
  1.4 43.5 %copy-start.2 = (bf16[1024,384]{1,0:T(8,128)(2,1)S(1)}, bf16[1024,384]{1,0:T(8,128)(2,1)}, u32[]{:S(2)}) copy-start(bf16[1024,384]{1,0:T(8,128)(2,1)} %v_ref.3) | copy-start | bytes 2359300
  35.5 14.2 %copy-start = (bf16[16,16,1152]{2,1,0:T(8,128)(2,1)}, bf16[16,16,1152]{2,1,0:T(8,128)(2,1)S(1)}, u32[]{:S(2)}) copy-start(bf16[16,16,1152]{2,1,0:T(8,128)(2,1)S(1)} %all_to_all.15) | copy-start | bytes 1769476
  35.5 13.4 %collective-permute-start.2 = (bf16[256,384]{1,0:T(8,128)(2,1)S(1)}, bf16[256,384]{1,0:T(8,128)(2,1)S(1)}, u32[]{:S(2)}, u32[]{:S(2)}) collective-permute-start(bf16[256,384]{1,0:T(8,128)(2,1)S(1)} %slice.8.refs_0_), channel_id=1, source_target_pairs={{0,32},{16,48},{32,0},{48,16},{1,33},{17,49},{33,1},{49,17},{2,34}... | collective-permute-start | bytes 589832 | tf_op jit(solution)/shard_map/ppermute | solution.py:300
  40.2 8.7 %collective-permute-start.1 = (bf16[256,384]{1,0:T(8,128)(2,1)S(1)}, bf16[256,384]{1,0:T(8,128)(2,1)S(1)}, u32[]{:S(2)}, u32[]{:S(2)}) collective-permute-start(bf16[256,384]{1,0:T(8,128)(2,1)S(1)} %slice.8.refs_0_), channel_id=1, source_target_pairs={{0,48},{16,32},{32,16},{48,0},{1,49},{17,33},{33,17},{49,1},{2,50}... | collective-permute-start | bytes 589832 | tf_op jit(solution)/shard_map/ppermute | solution.py:300
  43.0 6.7 %collective-permute-start = (bf16[256,384]{1,0:T(8,128)(2,1)S(1)}, bf16[256,384]{1,0:T(8,128)(2,1)S(1)}, u32[]{:S(2)}, u32[]{:S(2)}) collective-permute-start(bf16[256,384]{1,0:T(8,128)(2,1)S(1)} %slice.8.refs_0_), channel_id=1, source_target_pairs={{0,16},{16,0},{32,48},{48,32},{1,17},{17,1},{33,49},{49,33},{2,18}... | collective-permute-start | bytes 589832 | tf_op jit(solution)/shard_map/ppermute | solution.py:300
  44.9 0.7 copy-start.4
  44.9 0.7 copy-start.5
  55.4 33.8 %all-to-all-start.1 = ((s16[64,56,128]{2,1,0:T(8,128)(2,1)}), s16[64,56,128]{2,1,0:T(8,128)(2,1)S(1)}, u32[]{:S(2)}, u32[]{:S(2)}) async-start(s16[64,56,128]{2,1,0:T(8,128)(2,1)} %attend.3.after_ref), calls=%async_computation.1 | async-start | bytes 1835008 | tf_op jit(solution)/shard_map/all_to_all | solution.py:324
  66.8 22.4 %copy-start.3 = (f32[50,384]{1,0:T(8,128)S(1)}, f32[50,384]{1,0:T(8,128)}, u32[]{:S(2)}) copy-start(f32[50,384]{1,0:T(8,128)} %gate_ref.1) | copy-start | bytes 230404
  68.7 34.7 %collective-permute-start.5 = (bf16[256,768]{1,0:T(8,128)(2,1)}, bf16[256,768]{1,0:T(8,128)(2,1)S(1)}, u32[]{:S(2)}, u32[]{:S(2)}) collective-permute-start(bf16[256,768]{1,0:T(8,128)(2,1)} %pick.1), channel_id=1, source_target_pairs={{0,32},{16,48},{32,0},{48,16},{1,33},{17,49},{33,1},{49,17},{2,34}... | collective-permute-start | bytes 1179656 | tf_op jit(solution)/shard_map/ppermute | solution.py:300
  73.2 30.2 %collective-permute-start.4 = (bf16[256,768]{1,0:T(8,128)(2,1)}, bf16[256,768]{1,0:T(8,128)(2,1)S(1)}, u32[]{:S(2)}, u32[]{:S(2)}) collective-permute-start(bf16[256,768]{1,0:T(8,128)(2,1)} %pick.1), channel_id=1, source_target_pairs={{0,48},{16,32},{32,16},{48,0},{1,49},{17,33},{33,17},{49,1},{2,50}... | collective-permute-start | bytes 1179656 | tf_op jit(solution)/shard_map/ppermute | solution.py:300
  75.9 27.5 %collective-permute-start.3 = (bf16[256,768]{1,0:T(8,128)(2,1)}, bf16[256,768]{1,0:T(8,128)(2,1)S(1)}, u32[]{:S(2)}, u32[]{:S(2)}) collective-permute-start(bf16[256,768]{1,0:T(8,128)(2,1)} %pick.1), channel_id=1, source_target_pairs={{0,16},{16,0},{32,48},{48,32},{1,17},{17,1},{33,49},{49,33},{2,18}... | collective-permute-start | bytes 1179656 | tf_op jit(solution)/shard_map/ppermute | solution.py:300
  90.8 16.8 %all-to-all-start.2 = ((f32[8,1,128]{2,1,0:T(1,128)}), f32[8,1,128]{2,1,0:T(1,128)S(1)}, u32[]{:S(2)}, u32[]{:S(2)}) async-start(f32[8,1,128]{2,1,0:T(1,128)} %get-tuple-element.12), calls=%async_computation.2 | async-start | bytes 8192 | tf_op jit(solution)/shard_map/all_to_all | solution.py:326
  103.4 0.8 copy-start.6
  103.4 0.9 copy-start.7
  103.5 1.0 copy-start.8
